TPU v7x, 32 devices: a whole 2x2x4 slice. The times are simulated.
32 devices in a mesh: blk: 16 (over z, y, x), tp: 2 (over core).
Axes of the slice: x: 2, y: 2, z: 4, core: 2. Of those that a mesh axis runs over, the one named last changes fastest.
Arguments:
- tokens: bfloat16 [2, 2048, 1024], P(None, 'blk'), may hold values from -6 to 6
- memory: bfloat16 [9408, 1024], P('blk'), may hold values from -6 to 6
- segment_ids: int32 [2, 2048], P(None, 'blk'), may hold values from 0 to 2, as said below
- token_valid: int32 [2, 2048], P(None, 'blk'), may hold values from 0 to 1, as said below
- segment_page: int32 [2, 3], replicated, may hold values from 0 to 15
- gain_one: float32 [1024], replicated, may hold values from 0.5 to 1.5
- weight_query: bfloat16 [1024, 1024], P(None, 'tp'), may hold values from -0.1875 to 0.1875
- weight_key: bfloat16 [1024, 1024], P(None, 'tp'), may hold values from -0.1875 to 0.1875
- weight_value: bfloat16 [1024, 1024], P(None, 'tp'), may hold values from -0.1875 to 0.1875
- weight_out: bfloat16 [1024, 1024], P('tp'), may hold values from -1.5 to 1.5
- gain_two: float32 [1024], replicated, may hold values from 0.5 to 1.5
- cross_query: bfloat16 [1024, 1024], P(None, 'tp'), may hold values from -0.1875 to 0.1875
- cross_key: bfloat16 [1024, 1024], P(None, 'tp'), may hold values from -0.1875 to 0.1875
- cross_value: bfloat16 [1024, 1024], P(None, 'tp'), may hold values from -0.1875 to 0.1875
- cross_out: bfloat16 [1024, 1024], P('tp'), may hold values from -0.75 to 0.75
- gain_three: float32 [1024], replicated, may hold values from 0.5 to 1.5
- weight_up: bfloat16 [1024, 4096], P(None, 'tp'), may hold values from -0.1875 to 0.1875
- weight_down: bfloat16 [4096, 1024], P('tp'), may hold values from -0.09375 to 0.09375
- cotangent: bfloat16 [2, 2048, 1024], P(None, 'blk'), may hold values from -6 to 6
Outputs:
- out: bfloat16 [2, 2048, 1024], P(None, 'blk')
- grad_input: float32 [2, 2048, 1024], P(None, 'blk')
- grad_memory: float32 [9408, 1024], P('blk')
- grad_weight_query: float32 [1024, 1024], P('blk', 'tp')
- grad_weight_key: float32 [1024, 1024], P('blk', 'tp')
- grad_weight_value: float32 [1024, 1024], P('blk', 'tp')
- grad_weight_out: float32 [1024, 1024], P('tp', 'blk')
- grad_cross_query: float32 [1024, 1024], P('blk', 'tp')
- grad_cross_key: float32 [1024, 1024], P('blk', 'tp')
- grad_cross_value: float32 [1024, 1024], P('blk', 'tp')
- grad_cross_out: float32 [1024, 1024], P('tp', 'blk')
- grad_weight_up: float32 [1024, 4096], P('blk', 'tp')
- grad_weight_down: float32 [4096, 1024], P('tp', 'blk')
- grad_gain_one: float32 [1024], P('blk')
- grad_gain_two: float32 [1024], P('blk')
- grad_gain_three: float32 [1024], P('blk')
Inputs may be any that keep to these rules, and one draw needn't show every extreme that they name: `segment_ids`: never falls along a packed row; each of the 3 segments of a row holds 1 to 1984 tokens, and one segment of every row holds exactly 1984. `token_valid`: 1 at the first token of every segment.
All inputs are finite; a program needn't handle non-finite values.
Results may differ from a plain program's by a relative error of at most 0.028.
Values may be sent and summed in bfloat16 or wider, within the bound.
A program may use at most 320 MiB of HBM per device.

v0:
```python
from functools import partial

import jax
import jax.numpy as jnp
from jax import lax
from jax.sharding import PartitionSpec as P

MEM_LEN = 588
HEAD_DIM = 64
NSEG = 3


EPS = 1e-05
NEG = -1e30


def product(left, right):
    return jnp.dot(left, right, preferred_element_type=jnp.float32)


def product_left(left, right):
    return lax.dot_general(
        left, right, (((0,), (0,)), ((), ())), preferred_element_type=jnp.float32
    )


def product_right(left, right):
    return lax.dot_general(
        left, right, (((1,), (1,)), ((), ())), preferred_element_type=jnp.float32
    )


def layer_norm(value, gain):
    mean = jnp.mean(value, axis=-1, keepdims=True)
    centred = value - mean
    inv_std = lax.rsqrt(jnp.mean(centred * centred, axis=-1, keepdims=True) + EPS)
    unit = centred * inv_std
    return (unit * gain, unit, inv_std)


def norm_back(grad, unit, inv_std, gain):
    scaled = grad * gain
    gain_grad = jnp.sum(grad * unit, axis=0)
    inner = (
        scaled
        - jnp.mean(scaled, axis=-1, keepdims=True)
        - unit * jnp.mean(scaled * unit, axis=-1, keepdims=True)
    )
    return (inner * inv_std, gain_grad)


def tp_total(partial_sum):
    return lax.psum(partial_sum.astype(jnp.bfloat16), "tp").astype(jnp.float32)


def allowed_pairs(query_segments, query_positions, key_segments, key_positions, key_valid):
    same = query_segments[..., :, None] == key_segments[..., None, :]
    causal = key_positions[None, :] <= query_positions[:, None]
    return same & causal & (key_valid[..., None, :] == 1)


def guarded(compute):
    return compute(0)


def head_scores(query, keys, scale):
    return jnp.einsum("qhd,khd->hqk", query, keys, preferred_element_type=jnp.float32) * scale


def forward_block(state, query, keys, values, allowed, scale):

    def compute(unused):
        largest, weight_sum, weighted = state
        allowed_heads = allowed[:, None]
        scores = (
            jnp.einsum("pqhd,pkhd->phqk", query, keys, preferred_element_type=jnp.float32) * scale
        )
        scores = jnp.where(allowed_heads, scores, NEG)
        new_largest = jnp.maximum(largest, jnp.max(scores, axis=-1))
        weights = jnp.where(allowed_heads, jnp.exp(scores - new_largest[..., None]), 0.0)
        weight_sum = jnp.sum(weights, axis=-1)
        update = jnp.einsum(
            "phqk,pkhd->phqd",
            weights.astype(jnp.bfloat16),
            values,
            preferred_element_type=jnp.float32,
        )
        return (new_largest, weight_sum, update)

    return guarded(compute)


def backward_block(query, grad_out, log_total, row_dot, keys, values, allowed, scale):

    def compute(unused):
        scores = head_scores(query, keys, scale)
        weights = jnp.where(allowed[None], jnp.exp(scores - log_total[..., None]), 0.0)
        value_grad = jnp.einsum(
            "hqk,qhd->khd",
            weights.astype(jnp.bfloat16),
            grad_out,
            preferred_element_type=jnp.float32,
        )
        weight_grad = jnp.einsum(
            "qhd,khd->hqk", grad_out, values, preferred_element_type=jnp.float32
        )
        score_grad = (weights * (weight_grad - row_dot[..., None])).astype(jnp.bfloat16)
        query_grad = jnp.einsum(
            "hqk,khd->qhd", score_grad, keys, preferred_element_type=jnp.float32
        )
        key_grad = jnp.einsum("hqk,qhd->khd", score_grad, query, preferred_element_type=jnp.float32)
        return (query_grad, key_grad, value_grad)

    return guarded(compute)


def cross_forward(query, page_keys, page_values, row_page, scale):
    rows, heads_here, head_size = query.shape

    def page_step(carry, item):
        output, log_total = carry
        keys, values, page = item
        on_page = row_page == page

        def compute(unused):
            scores = head_scores(query, keys, scale)
            largest = jnp.max(scores, axis=-1, keepdims=True)
            exp_scores = jnp.exp(scores - largest)
            weight_sum = jnp.sum(exp_scores, axis=-1, keepdims=True)
            weights = (exp_scores / weight_sum).astype(jnp.bfloat16)
            part_out = jnp.einsum(
                "hqk,khd->hqd", weights, values, preferred_element_type=jnp.float32
            )
            new_output = jnp.where(on_page[None, :, None], part_out, output)
            new_log = jnp.where(
                on_page[None, :], (largest + jnp.log(weight_sum))[..., 0], log_total
            )
            return (new_output, new_log)

        def keep(unused):
            return (output, log_total)

        return (lax.cond(jnp.any(on_page), compute, keep, 0), None)

    start_carry = (
        jnp.zeros((heads_here, rows, head_size), jnp.float32),
        jnp.zeros((heads_here, rows), jnp.float32),
    )
    pages = jnp.arange(page_keys.shape[0], dtype=jnp.int32)
    (output, log_total), unused = lax.scan(page_step, start_carry, (page_keys, page_values, pages))
    return (output, log_total)


def cross_backward(query, grad_out, page_keys, page_values, row_page, log_total, scale):

    def page_step(query_grad, item):
        keys, values, page = item
        on_page = row_page == page

        def compute(unused):
            scores = head_scores(query, keys, scale)
            weights = jnp.where(on_page[None, :, None], jnp.exp(scores - log_total[..., None]), 0.0)
            value_grad = jnp.einsum(
                "hqk,qhd->khd",
                weights.astype(jnp.bfloat16),
                grad_out,
                preferred_element_type=jnp.float32,
            )
            weight_grad = jnp.einsum(
                "qhd,khd->hqk", grad_out, values, preferred_element_type=jnp.float32
            )
            row_dot = jnp.sum(weights * weight_grad, axis=-1, keepdims=True)
            score_grad = (weights * (weight_grad - row_dot)).astype(jnp.bfloat16)
            query_add = jnp.einsum(
                "hqk,khd->qhd", score_grad, keys, preferred_element_type=jnp.float32
            )
            key_grad = jnp.einsum(
                "hqk,qhd->khd", score_grad, query, preferred_element_type=jnp.float32
            )
            return (query_grad + query_add, key_grad, value_grad)

        def empty(unused):
            return (
                query_grad,
                jnp.zeros(keys.shape, jnp.float32),
                jnp.zeros(values.shape, jnp.float32),
            )

        query_grad, key_grad, value_grad = lax.cond(jnp.any(on_page), compute, empty, 0)
        return (query_grad, (key_grad, value_grad))

    pages = jnp.arange(page_keys.shape[0], dtype=jnp.int32)
    start_grad = jnp.zeros(query.shape, jnp.float32)
    query_grad, (key_terms, value_terms) = lax.scan(
        page_step, start_grad, (page_keys, page_values, pages)
    )
    return (query_grad, key_terms, value_terms)


def group_rows(rows, count):
    factor = 1
    while count % (factor * 2) == 0 and rows * factor < 512:
        factor = factor * 2
    return rows * factor


def local(
    tokens,
    memory,
    segment_ids,
    token_valid,
    segment_page,
    gain_one,
    weight_query,
    weight_key,
    weight_value,
    weight_out,
    gain_two,
    cross_query,
    cross_key,
    cross_value,
    cross_out,
    gain_three,
    weight_up,
    weight_down,
    cotangent,
):
    packs, rows, width = tokens.shape
    local_width = weight_query.shape[1]
    heads_here = local_width // HEAD_DIM
    scale = HEAD_DIM ** (-0.5)
    count = lax.axis_size("blk")
    place = lax.axis_index("blk")
    total_rows = rows * count
    flat_rows = packs * rows
    slot_count = packs * NSEG
    positions = place * rows + jnp.arange(rows, dtype=jnp.int32)
    all_segments, all_valid = (
        lax.all_gather(segment_ids, "blk", axis=1, tiled=True),
        lax.all_gather(token_valid, "blk", axis=1, tiled=True),
    )

    def split(flat):
        return flat.reshape(flat.shape[:-1] + (heads_here, HEAD_DIM))

    def join(heads_first):
        return jnp.moveaxis(heads_first, -3, -2).reshape(-1, local_width)

    residual_in = tokens.reshape(flat_rows, width).astype(jnp.float32)
    normed_one, unit_one, inv_one = layer_norm(residual_in, gain_one)
    hidden_one = normed_one.astype(jnp.bfloat16)
    query_flat = product(hidden_one, weight_query).astype(jnp.bfloat16)
    key_flat = product(hidden_one, weight_key).astype(jnp.bfloat16)
    value_flat = product(hidden_one, weight_value).astype(jnp.bfloat16)
    query_heads = split(query_flat).reshape(packs, rows, heads_here, HEAD_DIM)
    key_packs = key_flat.reshape(packs, rows, local_width)
    value_packs = value_flat.reshape(packs, rows, local_width)

    def fold_keys(state, piece):
        keys, values = piece
        span = keys.shape[1]
        key_positions = jnp.arange(span, dtype=jnp.int32)
        allowed = allowed_pairs(segment_ids, positions, all_segments, key_positions, all_valid)
        return forward_block(state, query_heads, split(keys), split(values), allowed, scale)

    start_state = (
        jnp.full((packs, heads_here, rows), NEG, jnp.float32),
        jnp.zeros((packs, heads_here, rows), jnp.float32),
        jnp.zeros((packs, heads_here, rows, HEAD_DIM), jnp.float32),
    )
    largest, weight_sum, weighted = fold_keys(
        start_state,
        (
            lax.all_gather(key_packs, "blk", axis=1, tiled=True),
            lax.all_gather(value_packs, "blk", axis=1, tiled=True),
        ),
    )
    log_total = largest + jnp.log(weight_sum)
    attention = weighted / weight_sum[..., None]
    mixed = join(attention).astype(jnp.bfloat16)
    residual_one = residual_in + tp_total(product(mixed, weight_out))
    normed_two, unit_two, inv_two = layer_norm(residual_one, gain_two)
    hidden_two = normed_two.astype(jnp.bfloat16)
    cross_heads = split(product(hidden_two, cross_query).astype(jnp.bfloat16))
    own_keys = product(memory, cross_key).astype(jnp.bfloat16)
    own_values = product(memory, cross_value).astype(jnp.bfloat16)
    page_flat = segment_page.reshape(slot_count)
    slot_rows = (jnp.arange(packs, dtype=jnp.int32)[:, None] * NSEG + segment_ids).reshape(
        flat_rows
    )
    page_keys, page_values = (
        lax.all_gather(own_keys, "blk", axis=0, tiled=True),
        lax.all_gather(own_values, "blk", axis=0, tiled=True),
    )
    page_count = page_keys.shape[0] // MEM_LEN
    slots = jnp.arange(slot_count, dtype=jnp.int32)
    row_key = jnp.sum(
        jnp.where(slot_rows[:, None] == slots[None, :], page_flat[None, :], 0), axis=1
    )
    page_keys = page_keys.reshape(page_count, MEM_LEN, heads_here, HEAD_DIM)
    page_values = page_values.reshape(page_count, MEM_LEN, heads_here, HEAD_DIM)
    cross_attention, cross_log = cross_forward(cross_heads, page_keys, page_values, row_key, scale)
    cross_mixed = join(cross_attention).astype(jnp.bfloat16)
    residual_two = residual_one + tp_total(product(cross_mixed, cross_out))
    normed_three, unit_three, inv_three = layer_norm(residual_two, gain_three)
    hidden_three = normed_three.astype(jnp.bfloat16)
    up_value = product(hidden_three, weight_up)
    gelu_value, gelu_back = jax.vjp(partial(jax.nn.gelu, approximate=False), up_value)
    gelu_low = gelu_value.astype(jnp.bfloat16)
    result = residual_two + tp_total(product(gelu_low, weight_down))
    out = result.astype(jnp.bfloat16).reshape(packs, rows, width)
    grad_result = cotangent.reshape(flat_rows, width).astype(jnp.float32)
    down_in = grad_result.astype(jnp.bfloat16)
    grad_weight_down = product_left(gelu_low, down_in)
    up_grad = gelu_back(product_right(down_in, weight_down))[0].astype(jnp.bfloat16)
    grad_weight_up = product_left(hidden_three, up_grad)
    grad_hidden_three = tp_total(product_right(up_grad, weight_up))
    norm_grad, grad_gain_three = norm_back(grad_hidden_three, unit_three, inv_three, gain_three)
    grad_two = grad_result + norm_grad
    cross_in = grad_two.astype(jnp.bfloat16)
    grad_cross_out = product_left(cross_mixed, cross_in)
    cross_grad_heads = split(product_right(cross_in, cross_out).astype(jnp.bfloat16))
    cross_query_grad, page_key_terms, page_value_terms = cross_backward(
        cross_heads, cross_grad_heads, page_keys, page_values, row_key, cross_log, scale
    )
    cross_query_low = (cross_query_grad.reshape(flat_rows, local_width) * scale).astype(
        jnp.bfloat16
    )
    key_term_rows = page_key_terms.reshape(page_count * MEM_LEN, local_width) * scale
    value_term_rows = page_value_terms.reshape(page_count * MEM_LEN, local_width)
    own_key_grad, own_value_grad = (
        lax.psum_scatter(key_term_rows, "blk", scatter_dimension=0, tiled=True),
        lax.psum_scatter(value_term_rows, "blk", scatter_dimension=0, tiled=True),
    )
    own_key_low = own_key_grad.astype(jnp.bfloat16)
    own_value_low = own_value_grad.astype(jnp.bfloat16)
    grad_cross_key = product_left(memory, own_key_low)
    grad_cross_value = product_left(memory, own_value_low)
    grad_memory = tp_total(
        product_right(own_key_low, cross_key) + product_right(own_value_low, cross_value)
    )
    grad_cross_query = product_left(hidden_two, cross_query_low)
    grad_hidden_two = tp_total(product_right(cross_query_low, cross_query))
    norm_grad, grad_gain_two = norm_back(grad_hidden_two, unit_two, inv_two, gain_two)
    grad_one = grad_two + norm_grad
    self_in = grad_one.astype(jnp.bfloat16)
    grad_weight_out = product_left(mixed, self_in)
    mixed_grad = product_right(self_in, weight_out).astype(jnp.bfloat16)
    grad_heads = split(mixed_grad).reshape(packs, rows, heads_here, HEAD_DIM)
    row_dot = jnp.einsum("pqhd,phqd->phq", grad_heads.astype(jnp.float32), attention)
    span = group_rows(rows, count)
    groups = total_rows // span
    all_positions = jnp.arange(total_rows, dtype=jnp.int32).reshape(groups, span)
    zeros = jnp.zeros((rows, heads_here, HEAD_DIM), jnp.float32)
    query_parts, key_parts, value_parts = ([], [], [])
    for pack in range(packs):
        pack_queries = query_heads[pack]
        pack_grads = grad_heads[pack]
        pack_logs = log_total[pack]
        pack_dots = row_dot[pack]
        pack_segments = segment_ids[pack]
        all_keys, all_values = (
            lax.all_gather(key_packs[pack], "blk", axis=0, tiled=True),
            lax.all_gather(value_packs[pack], "blk", axis=0, tiled=True),
        )

        def key_group(query_grad, item):
            keys, values, key_segments, key_valid, key_positions = item
            allowed = allowed_pairs(
                pack_segments, positions, key_segments, key_positions, key_valid
            )
            query_add, key_add, value_add = backward_block(
                pack_queries,
                pack_grads,
                pack_logs,
                pack_dots,
                split(keys),
                split(values),
                allowed,
                scale,
            )
            return (query_grad + query_add, (key_add, value_add))

        items = (
            all_keys.reshape(groups, span, local_width),
            all_values.reshape(groups, span, local_width),
            all_segments[pack].reshape(groups, span),
            all_valid[pack].reshape(groups, span),
            all_positions,
        )
        query_grad, (key_terms, value_terms) = lax.scan(key_group, zeros, items)
        key_grad, value_grad = (
            lax.psum_scatter(
                key_terms.reshape(total_rows, local_width) * scale,
                "blk",
                scatter_dimension=0,
                tiled=True,
            ),
            lax.psum_scatter(
                value_terms.reshape(total_rows, local_width), "blk", scatter_dimension=0, tiled=True
            ),
        )
        query_parts.append(query_grad.reshape(rows, local_width) * scale)
        key_parts.append(key_grad)
        value_parts.append(value_grad)
    query_low = jnp.concatenate(query_parts, axis=0).astype(jnp.bfloat16)
    key_low = jnp.concatenate(key_parts, axis=0).astype(jnp.bfloat16)
    value_low = jnp.concatenate(value_parts, axis=0).astype(jnp.bfloat16)
    grad_weight_query = product_left(hidden_one, query_low)
    grad_weight_key = product_left(hidden_one, key_low)
    grad_weight_value = product_left(hidden_one, value_low)
    grad_hidden_one = tp_total(
        product_right(query_low, weight_query)
        + product_right(key_low, weight_key)
        + product_right(value_low, weight_value)
    )
    norm_grad, grad_gain_one = norm_back(grad_hidden_one, unit_one, inv_one, gain_one)
    grad_input = (grad_one + norm_grad).reshape(packs, rows, width)
    shares = (
        lax.psum_scatter(grad_weight_query, "blk", scatter_dimension=0, tiled=True),
        lax.psum_scatter(grad_weight_key, "blk", scatter_dimension=0, tiled=True),
        lax.psum_scatter(grad_weight_value, "blk", scatter_dimension=0, tiled=True),
        lax.psum_scatter(grad_weight_out, "blk", scatter_dimension=1, tiled=True),
        lax.psum_scatter(grad_cross_query, "blk", scatter_dimension=0, tiled=True),
        lax.psum_scatter(grad_cross_key, "blk", scatter_dimension=0, tiled=True),
        lax.psum_scatter(grad_cross_value, "blk", scatter_dimension=0, tiled=True),
        lax.psum_scatter(grad_cross_out, "blk", scatter_dimension=1, tiled=True),
        lax.psum_scatter(grad_weight_up, "blk", scatter_dimension=0, tiled=True),
        lax.psum_scatter(grad_weight_down, "blk", scatter_dimension=1, tiled=True),
        lax.psum_scatter(grad_gain_one, "blk", scatter_dimension=0, tiled=True),
        lax.psum_scatter(grad_gain_two, "blk", scatter_dimension=0, tiled=True),
        lax.psum_scatter(grad_gain_three, "blk", scatter_dimension=0, tiled=True),
    )
    return (out, grad_input, grad_memory) + tuple(shares)


def solution(mesh):
    in_specs = (
        P(None, "blk", None),
        P("blk", None),
        P(None, "blk"),
        P(None, "blk"),
        P(),
        P(),
        P(None, "tp"),
        P(None, "tp"),
        P(None, "tp"),
        P("tp", None),
        P(),
        P(None, "tp"),
        P(None, "tp"),
        P(None, "tp"),
        P("tp", None),
        P(),
        P(None, "tp"),
        P("tp", None),
        P(None, "blk", None),
    )
    out_specs = (
        P(None, "blk", None),
        P(None, "blk", None),
        P("blk", None),
        P("blk", "tp"),
        P("blk", "tp"),
        P("blk", "tp"),
        P("tp", "blk"),
        P("blk", "tp"),
        P("blk", "tp"),
        P("blk", "tp"),
        P("tp", "blk"),
        P("blk", "tp"),
        P("tp", "blk"),
        P("blk"),
        P("blk"),
        P("blk"),
    )
    return jax.shard_map(local, mesh=mesh, in_specs=in_specs, out_specs=out_specs, check_vma=False)
```

profile of v0, /device:TPU:0, one launch (start us, length us, event | category | flops | bytes accessed | tf_op | source)
XLA Modules:
  0.0 4668.7 jit_solution(1188903998650199454)
XLA Ops:
  17.2 42.5 all_gather.30
  59.7 35.7 all_gather.31
  118.5 52.1 %all-gather.13.cloned.1.call-done = bf16[2,2048,512]{2,1,0:T(8,128)(2,1)} async-done(((bf16[2,128,512]{2,1,0:T(8,128)(2,1)}), bf16[2,2048,512]{2,1,0:T(8,128)(2,1)}) %all-gather.13.cloned.1.call-update) | async-done | bytes 4194320 | tf_op jit(solution)/shard_map/all_gather | solution.py:275
  176.9 12.2 fusion.93
  196.6 12.3 all-reduce.15.cloned.1.call-done
  215.0 123.3 %all-gather.23.cloned.1.call-done = bf16[16,588,512]{2,1,0:T(8,128)(2,1)} async-done(((bf16[1,588,512]{2,1,0:T(8,128)(2,1)}), bf16[16,588,512]{2,1,0:T(8,128)(2,1)}) %all-gather.23.cloned.1.call-update) | async-done | bytes 9633808 | tf_op jit(solution)/shard_map/all_gather | solution.py:292
  338.4 14.2 copy.136
  352.5 112.3 %all-gather.25.cloned.1.call-done = bf16[16,588,512]{2,1,0:T(8,128)(2,1)} async-done(((bf16[1,588,512]{2,1,0:T(8,128)(2,1)}), bf16[16,588,512]{2,1,0:T(8,128)(2,1)}) %all-gather.25.cloned.1.call-update) | async-done | bytes 9633808 | tf_op jit(solution)/shard_map/all_gather | solution.py:293
  464.9 14.2 copy.138
  479.1 60.8 %while.59 = (s32[]{:T(128)}, bf16[8,256,64]{1,2,0:T(8,128)(2,1)S(1)}, f32[8,256]{1,0:T(8,128)S(1)}, s32[16]{0:T(128)S(1)}, s32[256]{0:T(256)S(1)}, /*index=5*/bf...) while((s32[]{:T(128)}, ...), condition=%wide.region_14.15_spmd, body=%wide.region_8.14_spmd.sunk | while | flops 319250944 | bytes 16624603 | solution.py:150
  542.6 16.9 all-reduce.17.cloned.1.call-done
  575.4 19.8 all-reduce.19.cloned.1.call-done
  601.2 567.3 %while.60 = (s32[]{:T(128)}, f32[256,8,64]{0,2,1:T(8,128)S(1)}, f32[16,588,8,64]{1,3,2,0:T(8,128)}, f32[16,588,8,64]{1,0,3,2:T(8,128)}, s32[16]{0:T(128)S(1)}, /...) while((s32[]{:T(128)}, f32[256,8,64]{0,2,1:T(8,128)S(1)}, ...), condition=%wide.region_27.28_spmd, body=%wide.region_22.27_spmd.sunk | while | flops 788896256 | bytes 51024148 | solution.py:194
  603.8 9.2 conditional.5
  616.6 26.9 dynamic_update_slice.34
  649.8 26.9 dynamic_update_slice.34
  683.0 26.9 dynamic_update_slice.34
  716.2 26.9 dynamic_update_slice.34
  749.4 26.9 dynamic_update_slice.34
  778.8 9.2 conditional.5
  791.6 26.9 dynamic_update_slice.34
  824.9 26.9 dynamic_update_slice.34
  858.1 26.9 dynamic_update_slice.34
  891.3 26.9 dynamic_update_slice.34
  920.7 9.2 conditional.5
  933.5 26.9 dynamic_update_slice.34
  966.7 26.9 dynamic_update_slice.34
  999.9 26.9 dynamic_update_slice.34
  1033.1 26.9 dynamic_update_slice.34
  1066.3 26.9 dynamic_update_slice.34
  1099.5 26.9 dynamic_update_slice.34
  1128.9 9.2 conditional.5
  1141.6 26.9 dynamic_update_slice.34
  1179.5 12.5 all-reduce.21.cloned.1.call-done
  1197.7 59.6 %all-gather.19.cloned.1.call-done = bf16[2048,512]{1,0:T(8,128)(2,1)} async-done(((bf16[128,512]{1,0:T(8,128)(2,1)}), bf16[2048,512]{1,0:T(8,128)(2,1)}) %all-gather.19.cloned.1.call-update) | async-done | bytes 2097168 | tf_op jit(solution)/shard_map/all_gather | solution.py:363
  1257.3 62.6 %all-gather.21.cloned.1.call-done = bf16[2048,512]{1,0:T(8,128)(2,1)} async-done(((bf16[128,512]{1,0:T(8,128)(2,1)}), bf16[2048,512]{1,0:T(8,128)(2,1)}) %all-gather.21.cloned.1.call-update) | async-done | bytes 2097168 | tf_op jit(solution)/shard_map/all_gather | solution.py:364
  1325.1 132.7 %while.62 = (s32[]{:T(128)}, f32[128,8,64]{0,2,1:T(8,128)}, f32[4,512,8,64]{1,3,2,0:T(8,128)}, f32[4,512,8,64]{1,0,3,2:T(4,128)}, bf16[4,512,512]{2,1,0:T(8,128)...) while((s32[]{:T(128)}, f32[128,8,64]{0,2,1:T(8,128)}, ...), condition=%wide.region_34.35_spmd.clone, body=%wide.region_33.34_spmd.clone.sunk | while | flops 339608192 | bytes 31613704 | solution.py:391
  1336.8 21.0 dynamic_update_slice.38
  1370.1 21.0 dynamic_update_slice.38
  1403.4 21.0 dynamic_update_slice.38
  1436.8 21.0 dynamic_update_slice.38
  1473.6 132.7 %while.61 = (s32[]{:T(128)}, f32[128,8,64]{0,2,1:T(8,128)}, f32[4,512,8,64]{1,3,2,0:T(8,128)}, f32[4,512,8,64]{1,0,3,2:T(4,128)}, bf16[4,512,512]{2,1,0:T(8,128)...) while((s32[]{:T(128)}, f32[128,8,64]{0,2,1:T(8,128)}, ...), condition=%wide.region_32.33_spmd.clone, body=%wide.region_31.32_spmd.clone.sunk | while | flops 339608192 | bytes 32138012 | solution.py:391
  1485.0 21.1 dynamic_update_slice.36
  1518.5 21.1 dynamic_update_slice.36
  1551.9 21.1 dynamic_update_slice.36
  1585.2 21.0 dynamic_update_slice.36
  1638.1 71.8 %reduce-scatter.21.cloned.1.call-done = f32[128,512]{0,1:T(8,128)} async-done(((f32[2048,512]{0,1:T(8,128)}), f32[128,512]{0,1:T(8,128)}) %reduce-scatter.21.cloned.1.call-update) | async-done | bytes 262160 | tf_op jit(solution)/shard_map/reduce_scatter | solution.py:393
  1711.5 95.3 %reduce-scatter.27.cloned.1.call-done = f32[128,512]{0,1:T(8,128)} async-done(((f32[2048,512]{0,1:T(8,128)}), f32[128,512]{0,1:T(8,128)}) %reduce-scatter.27.cloned.1.call-update) | async-done | bytes 262160 | tf_op jit(solution)/shard_map/reduce_scatter | solution.py:399
  1810.2 93.5 %reduce-scatter.25.cloned.1.call-done = f32[128,512]{0,1:T(8,128)} async-done(((f32[2048,512]{0,1:T(8,128)}), f32[128,512]{0,1:T(8,128)}) %reduce-scatter.25.cloned.1.call-update) | async-done | bytes 262160 | tf_op jit(solution)/shard_map/reduce_scatter | solution.py:399
  1908.2 8.9 broadcast_multiply_fusion
  1917.1 14.1 copy.153
  1931.2 22.4 mul.317
  1953.6 22.5 reshape.468
  1977.8 1649.5 %all-reduce.26 = (bf16[9408,512]{0,1:T(8,128)(2,1)}, bf16[9408,512]{0,1:T(8,128)(2,1)}, f32[1024]{0:T(1024)S(1)}, f32[1024]{0:T(1024)S(1)}, f32[1024]{0:T(1024)S(1)}) all-reduce(f32[9408,512]{0,1:T(8,128)} %mul.317, f32[9408,512]{0,1:T(8,128)} %reshape.468, ...), channel_id=6, replica_groups=mesh['blk'=16,'tp'=2] {'blk'}, use_global_device_ids=true, to_apply=%region_42.43.clone | all-reduce | flops 9636864 | bytes 57827328
  3685.4 50.4 %reduce-scatter.37.cloned.1.call-done = f32[64,512]{1,0:T(8,128)} async-done(((f32[1024,512]{1,0:T(8,128)}), f32[64,512]{1,0:T(8,128)}) %reduce-scatter.37.cloned.1.call-update) | async-done | bytes 131088 | tf_op jit(solution)/shard_map/reduce_scatter | solution.py:424
  3735.7 80.5 %reduce-scatter.39.cloned.1.call-done = f32[512,64]{0,1:T(8,128)} async-done(((f32[512,1024]{0,1:T(8,128)}), f32[512,64]{0,1:T(8,128)}) %reduce-scatter.39.cloned.1.call-update) | async-done | bytes 131088 | tf_op jit(solution)/shard_map/reduce_scatter | solution.py:427
  3816.2 80.6 %reduce-scatter.29.cloned.1.call-done = f32[64,512]{1,0:T(8,128)} async-done(((f32[1024,512]{1,0:T(8,128)}), f32[64,512]{1,0:T(8,128)}) %reduce-scatter.29.cloned.1.call-update) | async-done | bytes 131088 | tf_op jit(solution)/shard_map/reduce_scatter | solution.py:420
  3896.8 80.7 %reduce-scatter.35.cloned.1.call-done = f32[512,64]{0,1:T(8,128)} async-done(((f32[512,1024]{0,1:T(8,128)}), f32[512,64]{0,1:T(8,128)}) %reduce-scatter.35.cloned.1.call-update) | async-done | bytes 131088 | tf_op jit(solution)/shard_map/reduce_scatter | solution.py:423
  3977.5 80.8 %reduce-scatter.31.cloned.1.call-done = f32[64,512]{1,0:T(8,128)} async-done(((f32[1024,512]{1,0:T(8,128)}), f32[64,512]{1,0:T(8,128)}) %reduce-scatter.31.cloned.1.call-update) | async-done | bytes 131088 | tf_op jit(solution)/shard_map/reduce_scatter | solution.py:421
  4058.3 80.6 %reduce-scatter.33.cloned.1.call-done = f32[64,512]{1,0:T(8,128)} async-done(((f32[1024,512]{1,0:T(8,128)}), f32[64,512]{1,0:T(8,128)}) %reduce-scatter.33.cloned.1.call-update) | async-done | bytes 131088 | tf_op jit(solution)/shard_map/reduce_scatter | solution.py:422
  4138.9 80.7 %reduce-scatter.45.cloned.1.call-done = f32[64,512]{1,0:T(8,128)} async-done(((f32[1024,512]{1,0:T(8,128)}), f32[64,512]{1,0:T(8,128)}) %reduce-scatter.45.cloned.1.call-update) | async-done | bytes 131088
  4219.7 80.5 %reduce-scatter.47.cloned.1.call-done = f32[64,512]{1,0:T(8,128)} async-done(((f32[1024,512]{1,0:T(8,128)}), f32[64,512]{1,0:T(8,128)}) %reduce-scatter.47.cloned.1.call-update) | async-done | bytes 131088
  4300.2 177.9 %reduce-scatter.41.cloned.1.call-done = f32[64,2048]{1,0:T(8,128)} async-done(((f32[1024,2048]{1,0:T(8,128)}), f32[64,2048]{1,0:T(8,128)}) %reduce-scatter.41.cloned.1.call-update) | async-done | bytes 524304 | tf_op jit(solution)/shard_map/reduce_scatter | solution.py:428
  4478.1 183.3 %reduce-scatter.43.cloned.1.call-done = f32[2048,64]{0,1:T(8,128)} async-done(((f32[2048,1024]{0,1:T(8,128)}), f32[2048,64]{0,1:T(8,128)}) %reduce-scatter.43.cloned.1.call-update) | async-done | bytes 524304 | tf_op jit(solution)/shard_map/reduce_scatter | solution.py:429
  (701 shorter events, 507.8 us)
Async XLA Ops:
  7.2 184.3 %copy-start = (bf16[588,1024]{1,0:T(8,128)(2,1)S(1)}, bf16[588,1024]{1,0:T(8,128)(2,1)}, u32[]{:S(2)}) copy-start(bf16[588,1024]{1,0:T(8,128)(2,1)} %param.32) | copy-start | bytes 3612676
  7.2 89.0 %all-gather.11.cloned.1.call-start = ((), (), s32[]{:S(2)}) async-start(), calls=%async_computation.14 | async-start | bytes 4456448 | tf_op jit(solution)/shard_map/all_gather | solution.py:274
  13.9 45.7 copy-start.84
  14.0 156.6 %all-gather.13.cloned.1.call-start = ((), (), s32[]{:S(2)}) async-start(), calls=%async_computation.15 | async-start | bytes 4456448 | tf_op jit(solution)/shard_map/all_gather | solution.py:275
  16.4 192.5 %all-reduce.15.cloned.1.call-start = ((), (), s32[]{:S(2)}) async-start(), calls=%async_computation.16 | async-start | bytes 1048576 | tf_op jit(solution)/shard_map/psum | solution.py:53
  16.9 85.7 %copy-start.35 = (bf16[256,512]{1,0:T(8,128)(2,1)}, bf16[256,512]{1,0:T(8,128)(2,1)S(1)}, u32[]{:S(2)}) copy-start(bf16[256,512]{1,0:T(8,128)(2,1)S(1)} %convolution_convert_fusion.12) | copy-start | bytes 786436
  59.7 42.9 copy-start.59
  118.5 58.4 %copy-start.63 = (f32[2,8,128]{2,1,0:T(8,128)}, f32[2,8,128]{2,1,0:T(8,128)S(1)}, u32[]{:S(2)}) copy-start(f32[2,8,128]{2,1,0:T(8,128)S(1)} %fusion.48) | copy-start | bytes 24580
  176.9 13.2 copy-start.30
  191.4 147.0 %all-gather.23.cloned.1.call-start = ((), (), s32[]{:S(2)}) async-start(), calls=%async_computation.37 | async-start | bytes 10305536 | tf_op jit(solution)/shard_map/all_gather | solution.py:292
  194.4 14.5 copy-start.4
  194.4 270.4 %all-gather.25.cloned.1.call-start = ((), (), s32[]{:S(2)}) async-start(), calls=%async_computation.38 | async-start | bytes 10305536 | tf_op jit(solution)/shard_map/all_gather | solution.py:293
  196.3 16.5 copy-start.29
  196.3 16.5 copy-start.67
  196.3 363.3 %all-reduce.17.cloned.1.call-start = ((), (), s32[]{:S(2)}) async-start(), calls=%async_computation.17 | async-start | bytes 1048576 | tf_op jit(solution)/shard_map/psum | solution.py:53
  540.0 20.9 copy-start.39
  542.5 18.6 copy-start.57
  542.6 52.6 %all-reduce.19.cloned.1.call-start = ((), (), s32[]{:S(2)}) async-start(), calls=%async_computation.18 | async-start | bytes 1048576 | tf_op jit(solution)/shard_map/psum | solution.py:53
  560.9 36.5 copy-start.71
  561.2 36.2 copy-start.73
  573.0 22.2 copy-start.7
  575.1 616.9 %all-reduce.21.cloned.1.call-start = ((), (), s32[]{:S(2)}) async-start(), calls=%async_computation.19 | async-start | bytes 1048576 | tf_op jit(solution)/shard_map/psum | solution.py:53
  1168.5 8.4 copy-start.62
  1169.3 10.2 copy-start.64
  1169.3 10.2 copy-start.66
  1169.3 22.7 copy-start.10
  1169.3 22.7 copy-start.68
  1171.9 21.7 copy-start.15
  1171.9 21.7 copy-start.83
  1171.9 85.4 %all-gather.19.cloned.1.call-start = ((), (), s32[]{:S(2)}) async-start(), calls=%async_computation.22 | async-start | bytes 2228224 | tf_op jit(solution)/shard_map/all_gather | solution.py:363
  1173.7 146.1 %all-gather.21.cloned.1.call-start = ((), (), s32[]{:S(2)}) async-start(), calls=%async_computation.23 | async-start | bytes 2228224 | tf_op jit(solution)/shard_map/all_gather | solution.py:364
  1175.5 292.9 %all-gather.15.cloned.1.call-start = ((), (), s32[]{:S(2)}) async-start(), calls=%async_computation.20 | async-start | bytes 2228224 | tf_op jit(solution)/shard_map/all_gather | solution.py:363
  1176.2 292.1 %all-gather.17.cloned.1.call-start = ((), (), s32[]{:S(2)}) async-start(), calls=%async_computation.21 | async-start | bytes 2228224 | tf_op jit(solution)/shard_map/all_gather | solution.py:364
  1176.8 459.6 %reduce-scatter.23.cloned.1.call-start = ((), (), s32[]{:S(2)}) async-start(), calls=%async_computation.25 | async-start | bytes 4456448 | tf_op jit(solution)/shard_map/reduce_scatter | solution.py:393
  1335.7 22.1 copy-start.25
  1369.0 22.1 copy-start.25
  1402.3 22.1 copy-start.25
  1435.7 22.1 copy-start.25
  1467.2 242.6 %reduce-scatter.21.cloned.1.call-start = ((), (), s32[]{:S(2)}) async-start(), calls=%async_computation.24 | async-start | bytes 4456448 | tf_op jit(solution)/shard_map/reduce_scatter | solution.py:393
  1483.9 22.2 copy-start.27
  1517.4 22.2 copy-start.27
  1550.8 22.2 copy-start.27
  1584.1 22.1 copy-start.27
  1615.6 191.1 %reduce-scatter.27.cloned.1.call-start = ((), (), s32[]{:S(2)}) async-start(), calls=%async_computation.27 | async-start | bytes 4456448 | tf_op jit(solution)/shard_map/reduce_scatter | solution.py:399
  1621.9 281.7 %reduce-scatter.25.cloned.1.call-start = ((), (), s32[]{:S(2)}) async-start(), calls=%async_computation.26 | async-start | bytes 4456448 | tf_op jit(solution)/shard_map/reduce_scatter | solution.py:399
  1628.3 347.8 %all-reduce.23.cloned.1.call-start = ((), (), s32[]{:S(2)}) async-start(), calls=%async_computation.28 | async-start | bytes 1048576 | tf_op jit(solution)/shard_map/psum | solution.py:53
  1635.2 172.6 %copy-start.34 = (bf16[1024,512]{1,0:T(8,128)(2,1)S(1)}, bf16[1024,512]{1,0:T(8,128)(2,1)}, u32[]{:S(2)}) copy-start(bf16[1024,512]{1,0:T(8,128)(2,1)} %param.38) | copy-start | bytes 3145732
  1908.1 1773.2 %all-reduce.25.cloned.1.call-start = ((), (), s32[]{:S(2)}) async-start(), calls=%async_computation.41 | async-start | bytes 3473408 | tf_op jit(solution)/shard_map/psum | solution.py:53
  1953.6 22.5 copy-start.5
  1953.6 22.5 copy-start.70
  1953.6 22.5 copy-start.79
  1953.6 22.5 copy-start.81
  1953.6 24.1 copy-start.75
  1977.7 1649.5 %copy-start.50 = (bf16[1024,512]{1,0:T(8,128)(2,1)S(1)}, bf16[1024,512]{1,0:T(8,128)(2,1)}, u32[]{:S(2)}) copy-start(bf16[1024,512]{1,0:T(8,128)(2,1)} %param.43) | copy-start | bytes 3145732
  3633.5 102.2 %reduce-scatter.37.cloned.1.call-start = ((), (), s32[]{:S(2)}) async-start(), calls=%async_computation.33 | async-start | bytes 2228224 | tf_op jit(solution)/shard_map/reduce_scatter | solution.py:424
  3635.4 180.8 %reduce-scatter.39.cloned.1.call-start = ((), (), s32[]{:S(2)}) async-start(), calls=%async_computation.34 | async-start | bytes 2228224 | tf_op jit(solution)/shard_map/reduce_scatter | solution.py:427
  3639.6 257.2 %reduce-scatter.29.cloned.1.call-start = ((), (), s32[]{:S(2)}) async-start(), calls=%async_computation.29 | async-start | bytes 2228224 | tf_op jit(solution)/shard_map/reduce_scatter | solution.py:420
  3642.6 334.9 %reduce-scatter.35.cloned.1.call-start = ((), (), s32[]{:S(2)}) async-start(), calls=%async_computation.32 | async-start | bytes 2228224 | tf_op jit(solution)/shard_map/reduce_scatter | solution.py:423
  3645.4 412.9 %reduce-scatter.31.cloned.1.call-start = ((), (), s32[]{:S(2)}) async-start(), calls=%async_computation.30 | async-start | bytes 2228224 | tf_op jit(solution)/shard_map/reduce_scatter | solution.py:421
  3648.3 490.6 %reduce-scatter.33.cloned.1.call-start = ((), (), s32[]{:S(2)}) async-start(), calls=%async_computation.31 | async-start | bytes 2228224 | tf_op jit(solution)/shard_map/reduce_scatter | solution.py:422
  3650.2 569.5 %reduce-scatter.45.cloned.1.call-start = ((), (), s32[]{:S(2)}) async-start(), calls=%async_computation.39 | async-start | bytes 2228224
  3656.7 643.5 %reduce-scatter.47.cloned.1.call-start = ((), (), s32[]{:S(2)}) async-start(), calls=%async_computation.40 | async-start | bytes 2228224
  3663.3 814.8 %reduce-scatter.41.cloned.1.call-start = ((), (), s32[]{:S(2)}) async-start(), calls=%async_computation.35 | async-start | bytes 8912896 | tf_op jit(solution)/shard_map/reduce_scatter | solution.py:428
  3669.4 992.0 %reduce-scatter.43.cloned.1.call-start = ((), (), s32[]{:S(2)}) async-start(), calls=%async_computation.36 | async-start | bytes 8912896 | tf_op jit(solution)/shard_map/reduce_scatter | solution.py:429
  (72 other events, 225.7 us)
Sparse Core Ops, SparseCore 0:
  14.1 79.0 all-gather.10
  95.9 74.5 all-gather.12
  191.5 17.3 all-reduce.14
  212.3 125.9 all-gather.22
  341.8 122.9 all-gather.24
  542.7 16.8 all-reduce.16
  575.2 19.8 all-reduce.18
  1172.0 19.9 all-reduce.20
  1195.4 61.8 all-gather.18
  1260.5 59.3 all-gather.20
  1323.2 59.3 all-gather.14
  1385.8 59.3 all-gather.16
  1467.3 94.0 reduce-scatter.22
  1615.7 94.0 reduce-scatter.20
  1712.0 94.7 reduce-scatter.26
  1808.9 94.7 reduce-scatter.24
  1908.2 18.3 all-reduce.22
  3633.6 17.4 all-reduce.24
  3654.1 81.5 reduce-scatter.36
  3738.5 77.6 reduce-scatter.38
  3819.2 77.5 reduce-scatter.28
  3899.7 77.6 reduce-scatter.34
  3980.4 77.8 reduce-scatter.30
  4061.1 77.7 reduce-scatter.32
  4141.9 77.7 reduce-scatter.44
  4222.5 77.6 reduce-scatter.46
  4303.0 175.0 reduce-scatter.40
  4481.1 180.2 reduce-scatter.42
where the time goes:
time: 4700 us; the launch traced here: 4670 us
  blocking collectives  1730 us (37%)
  waiting for transfers between devices  1710 us (36%)
  local copies, waits for them, and re-layouts  871 us (19%)
  matrix products  215 us (5%)
  other arithmetic  102 us (2%)
    unnamed x1, blocking collectives  1650 us
    dynamic_update_slice x48, local copies, waits for them, and re-layouts, cross_backward(): lax.scan(page_step, start_grad, (page_keys, page_values, pages))  488 us
    reduce_scatter x2, waiting for transfers between devices, local(): lax.psum_scatter(value_terms.reshape(total_rows, local_width), 'blk', sca...  189 us
    reduce_scatter x1, waiting for transfers between devices, local(): lax.psum_scatter(grad_weight_down, 'blk', scatter_dimension=1, tiled=True)  183 us
    reduce_scatter x1, waiting for transfers between devices, local(): lax.psum_scatter(grad_weight_up, 'blk', scatter_dimension=0, tiled=True)  178 us
    dynamic_update_slice x16, local copies, waits for them, and re-layouts, local(): query_grad, (key_terms, value_terms) = lax.scan(key_group, zeros, items)  177 us
    unnamed x30, waiting for transfers between devices  163 us
    all_gather x1, waiting for transfers between devices, local(): lax.all_gather(own_keys, 'blk', axis=0, tiled=True)  123 us
  transfers between devices with their start and end apart: 28, of which 22 were waited for; matrix products, arithmetic and copies ran while one was open for 10% of the time, Pallas kernels for 0%

commit v1 on v0

v1 whole, which is shorter than its diff:
```python
import functools

import jax
import jax.numpy as jnp
from jax import lax
from jax.experimental import pallas as pl
from jax.experimental.pallas import tpu as pltpu
from jax.sharding import PartitionSpec as P

MEM_LEN = 588
HEAD_DIM = 64
NSEG = 3
EPS = 1e-05
NEG = -1e30
EXP2_SCALE = HEAD_DIM**-0.5 * 1.4426950408889634
SCALE = HEAD_DIM**-0.5
LANES = 128
BF16 = jnp.bfloat16
F32 = jnp.float32
MESH = pl.DeviceIdType.MESH
VMEM_LIMIT = 56 * 1024 * 1024


def dot(left, right, contract_left, contract_right):
    return lax.dot_general(
        left, right, (((contract_left,), (contract_right,)), ((), ())), preferred_element_type=F32
    )


def exchange(collective_id, items):
    count = len(items)
    most = max(item[2] for item in items)

    def body(*refs):
        sources, targets = refs[:count], refs[count : 2 * count]
        send_sem, recv_sem, own_sem = refs[2 * count :]
        me = lax.axis_index("blk")
        barrier = pltpu.get_barrier_semaphore()
        for offset in range(1, most):
            pl.semaphore_signal(
                barrier, inc=1, device_id={"blk": me ^ offset}, device_id_type=MESH
            )
        pl.semaphore_wait(barrier, most - 1)
        copies = []
        for offset in range(1, most):
            for index, (_, _, group, source, target) in enumerate(items):
                if offset >= group:
                    continue
                peer = me ^ offset
                copy = pltpu.make_async_remote_copy(
                    src_ref=source(sources[index], peer),
                    dst_ref=target(targets[index], me),
                    send_sem=send_sem.at[index, offset],
                    recv_sem=recv_sem.at[index, offset],
                    device_id={"blk": peer},
                    device_id_type=MESH,
                )
                copy.start()
                copies.append(copy)
        for index, (_, _, group, source, target) in enumerate(items):
            copy = pltpu.make_async_copy(
                source(sources[index], me), target(targets[index], me), own_sem.at[index]
            )
            copy.start()
            copies.append(copy)
        for copy in copies:
            copy.wait()

    outs = pl.pallas_call(
        body,
        out_shape=[jax.ShapeDtypeStruct(item[1], item[0].dtype) for item in items],
        in_specs=[pl.BlockSpec(memory_space=pl.ANY)] * count,
        out_specs=[pl.BlockSpec(memory_space=pl.ANY)] * count,
        scratch_shapes=[
            pltpu.SemaphoreType.DMA((count, most)),
            pltpu.SemaphoreType.DMA((count, most)),
            pltpu.SemaphoreType.DMA((count,)),
        ],
        compiler_params=pltpu.CompilerParams(collective_id=collective_id, has_side_effects=True),
    )(*[item[0] for item in items])
    return outs


class Layout:
    def __init__(self, count, packs, heads, rows, mem_rows):
        self.count, self.packs, self.heads, self.rows = count, packs, heads, rows
        self.half = count // packs
        self.parts = self.half // heads
        self.mem_rows = mem_rows
        self.mem_pad = -(-mem_rows // LANES) * LANES
        self.pieces = MEM_LEN // mem_rows
        self.pages_half = self.half // self.pieces

    def head(self, device):
        return lax.rem(device, self.half) // self.parts

    def to_units(self, value):
        def source(ref, peer):
            return ref.at[
                :,
                pl.ds(self.head(peer) * HEAD_DIM, HEAD_DIM),
                pl.ds((peer // self.half) * self.rows, self.rows),
            ]

        def target(ref, me):
            return ref.at[:, :, pl.ds(me * self.rows, self.rows)]

        shape = (value.shape[0], HEAD_DIM, self.count * self.rows)
        return (value, shape, self.count, source, target)

    def codes_to_units(self, value):
        def source(ref, peer):
            return ref.at[peer // self.half]

        def target(ref, me):
            return ref.at[:, pl.ds(me * self.rows, self.rows)]

        return (value, (value.shape[1], self.count * self.rows), self.count, source, target)

    def from_units(self, value):
        def source(ref, peer):
            return ref.at[:, :, pl.ds(peer * self.rows, self.rows)]

        def target(ref, me):
            return ref.at[
                lax.rem(me, self.parts),
                :,
                pl.ds(self.head(me) * HEAD_DIM, HEAD_DIM),
                pl.ds((me // self.half) * self.rows, self.rows),
            ]

        shape = (self.parts, value.shape[0], self.heads * HEAD_DIM, self.packs * self.rows)
        return (value, shape, self.count, source, target)

    def memory_to_units(self, value):
        def source(ref, peer):
            return ref.at[:, pl.ds(self.head(peer) * HEAD_DIM, HEAD_DIM), :]

        def target(ref, me):
            return ref.at[lax.rem(me, self.half)]

        return (value, (self.half, 2, HEAD_DIM, self.mem_pad), self.half, source, target)

    def memory_from_units(self, value):
        def source(ref, peer):
            return ref.at[lax.rem(peer, self.half)]

        def target(ref, me):
            return ref.at[
                lax.rem(me, self.parts), :, pl.ds(self.head(me) * HEAD_DIM, HEAD_DIM), :
            ]

        shape = (self.parts, 2, self.heads * HEAD_DIM, self.mem_pad)
        return (value, shape, self.half, source, target)


def self_forward_body(block, parts, q_ref, k_ref, v_ref, code_ref, qseg_ref, qpos_ref, *rest):
    out_ref, low_ref, log_ref, key_ref = rest
    step = pl.program_id(0)

    @pl.when(step == 0)
    def _():
        key_ref[...] = k_ref[0].T

    query = q_ref[0]
    width = query.shape[1]
    segments, positions = qseg_ref[...], qpos_ref[...]

    def fold(index, state, causal):
        largest, total, weighted = state
        start = pl.multiple_of(index * block, block)
        scores = jnp.dot(key_ref[pl.ds(start, block), :], query, preferred_element_type=F32)
        allowed = code_ref[pl.ds(start, block), :] == segments
        if causal:
            places = start + lax.broadcasted_iota(jnp.int32, (block, width), 0)
            allowed = allowed & (places <= positions)
        scores = jnp.where(allowed, scores, NEG)
        new = jnp.maximum(largest, jnp.max(scores, axis=0, keepdims=True))
        weights = jnp.exp2((scores - new) * EXP2_SCALE)
        keep = jnp.exp2((largest - new) * EXP2_SCALE)
        total = total * keep + jnp.sum(weights, axis=0, keepdims=True)
        update = jnp.dot(
            v_ref[0, :, pl.ds(start, block)], weights.astype(BF16), preferred_element_type=F32
        )
        return (new, total, weighted * keep + update)

    state = (
        jnp.full((1, width), NEG, F32),
        jnp.zeros((1, width), F32),
        jnp.zeros((HEAD_DIM, width), F32),
    )
    state = lax.fori_loop(0, step * parts, lambda i, s: fold(i, s, False), state)
    for part in range(parts):
        state = fold(step * parts + part, state, True)
    largest, total, weighted = state
    result = weighted / total
    out_ref[...] = result
    low_ref[0] = result.astype(BF16)
    log_ref[...] = largest * EXP2_SCALE + jnp.log2(total)


def self_forward(query, qkv, code, qseg, qpos, parts):
    total, width = qkv.shape[2], query.shape[2]
    block = min(512, width)
    row = pl.BlockSpec((1, block), lambda i: (0, i))
    return pl.pallas_call(
        functools.partial(self_forward_body, block, parts),
        grid=(width // block,),
        in_specs=[
            pl.BlockSpec((1, HEAD_DIM, block), lambda i: (0, 0, i)),
            pl.BlockSpec((1, HEAD_DIM, total), lambda i: (1, 0, 0)),
            pl.BlockSpec((1, HEAD_DIM, total), lambda i: (2, 0, 0)),
            pl.BlockSpec((total, 1), lambda i: (0, 0)),
            row,
            row,
        ],
        out_specs=[
            pl.BlockSpec((HEAD_DIM, block), lambda i: (0, i)),
            pl.BlockSpec((1, HEAD_DIM, block), lambda i: (0, 0, i)),
            row,
        ],
        out_shape=[
            jax.ShapeDtypeStruct((HEAD_DIM, width), F32),
            jax.ShapeDtypeStruct((1, HEAD_DIM, width), BF16),
            jax.ShapeDtypeStruct((1, width), F32),
        ],
        scratch_shapes=[pltpu.VMEM((total, HEAD_DIM), BF16)],
        compiler_params=pltpu.CompilerParams(vmem_limit_bytes=VMEM_LIMIT),
    )(query, qkv, qkv, code, qseg, qpos)


def self_backward_body(block, parts, q_ref, k_ref, v_ref, code_ref, qseg_ref, qpos_ref, *rest):
    grad_ref, out_ref, log_ref, dq_ref, dkv_ref, key_ref, value_ref, dk_ref, dv_ref = rest
    step = pl.program_id(0)

    @pl.when(step == 0)
    def _():
        key_ref[...] = k_ref[0].T
        value_ref[...] = v_ref[0].T
        dk_ref[...] = jnp.zeros_like(dk_ref)
        dv_ref[...] = jnp.zeros_like(dv_ref)

    query, grad = q_ref[0], grad_ref[0]
    width = query.shape[1]
    segments, positions, logs = qseg_ref[...], qpos_ref[...], log_ref[...]
    row_dot = jnp.sum(grad.astype(F32) * out_ref[...], axis=0, keepdims=True)

    def fold(index, dq, causal):
        start = pl.multiple_of(index * block, block)
        here = pl.ds(start, block)
        scores = jnp.dot(key_ref[here, :], query, preferred_element_type=F32)
        allowed = code_ref[here, :] == segments
        if causal:
            places = start + lax.broadcasted_iota(jnp.int32, (block, width), 0)
            allowed = allowed & (places <= positions)
        weights = jnp.where(allowed, jnp.exp2(scores * EXP2_SCALE - logs), 0.0)
        weight_grad = jnp.dot(value_ref[here, :], grad, preferred_element_type=F32)
        score_grad = (weights * (weight_grad - row_dot)).astype(BF16)
        dv_ref[:, here] += dot(grad, weights.astype(BF16), 1, 1)
        dk_ref[:, here] += dot(query, score_grad, 1, 1)
        return dq + jnp.dot(k_ref[0, :, here], score_grad, preferred_element_type=F32)

    dq = jnp.zeros((HEAD_DIM, width), F32)
    dq = lax.fori_loop(0, step * parts, lambda i, s: fold(i, s, False), dq)
    for part in range(parts):
        dq = fold(step * parts + part, dq, True)
    dq_ref[0] = (dq * SCALE).astype(BF16)

    @pl.when(step == pl.num_programs(0) - 1)
    def _():
        dkv_ref[0] = (dk_ref[...] * SCALE).astype(BF16)
        dkv_ref[1] = dv_ref[...].astype(BF16)


def self_backward(query, qkv, code, qseg, qpos, grad, out, log, parts):
    total, width = qkv.shape[2], query.shape[2]
    block = min(512, width)
    row = pl.BlockSpec((1, block), lambda i: (0, i))
    column = pl.BlockSpec((1, HEAD_DIM, block), lambda i: (0, 0, i))
    return pl.pallas_call(
        functools.partial(self_backward_body, block, parts),
        grid=(width // block,),
        in_specs=[
            column,
            pl.BlockSpec((1, HEAD_DIM, total), lambda i: (1, 0, 0)),
            pl.BlockSpec((1, HEAD_DIM, total), lambda i: (2, 0, 0)),
            pl.BlockSpec((total, 1), lambda i: (0, 0)),
            row,
            row,
            column,
            pl.BlockSpec((HEAD_DIM, block), lambda i: (0, i)),
            row,
        ],
        out_specs=[column, pl.BlockSpec((2, HEAD_DIM, total), lambda i: (0, 0, 0))],
        out_shape=[
            jax.ShapeDtypeStruct((1, HEAD_DIM, width), BF16),
            jax.ShapeDtypeStruct((2, HEAD_DIM, total), BF16),
        ],
        scratch_shapes=[
            pltpu.VMEM((total, HEAD_DIM), BF16),
            pltpu.VMEM((total, HEAD_DIM), BF16),
            pltpu.VMEM((HEAD_DIM, total), F32),
            pltpu.VMEM((HEAD_DIM, total), F32),
        ],
        compiler_params=pltpu.CompilerParams(vmem_limit_bytes=VMEM_LIMIT),
    )(query, qkv, qkv, code, qseg, qpos, grad, out, log)


def page_rows(span, piece, real):
    places = lax.broadcasted_iota(jnp.int32, (span, 1), 0)
    return lax.rem(places, piece) < real


def cross_forward_body(piece, real, low_ref, high_ref, q_ref, kv_ref, qseg_ref, *rest):
    out_ref, outlow_ref, log_ref, key_ref = rest
    step = pl.program_id(0)

    @pl.when(step == 0)
    def _():
        for slot in range(NSEG):
            key_ref[slot] = kv_ref[slot, 0].T

    query, segments = q_ref[0], qseg_ref[...]
    width, span = query.shape[1], kv_ref.shape[3]
    present = page_rows(span, piece, real)

    def fold(slot, state):
        logs, result = state
        scores = jnp.dot(key_ref[slot], query, preferred_element_type=F32)
        scores = jnp.where(present, scores, NEG)
        largest = jnp.max(scores, axis=0, keepdims=True)
        weights = jnp.exp2((scores - largest) * EXP2_SCALE)
        total = jnp.sum(weights, axis=0, keepdims=True)
        part = jnp.dot(kv_ref[slot, 1], weights.astype(BF16), preferred_element_type=F32) / total
        mine = segments == slot
        return (
            jnp.where(mine, largest * EXP2_SCALE + jnp.log2(total), logs),
            jnp.where(mine, part, result),
        )

    state = (jnp.zeros((1, width), F32), jnp.zeros((HEAD_DIM, width), F32))
    logs, result = lax.fori_loop(low_ref[step], high_ref[step] + 1, fold, state)
    out_ref[...] = result
    outlow_ref[0] = result.astype(BF16)
    log_ref[...] = logs


def cross_forward(query, kv, qseg, low, high, piece, real):
    width, span = query.shape[2], kv.shape[3]
    block = min(512, width)
    row = pl.BlockSpec((1, block), lambda i, *_: (0, i))
    column = pl.BlockSpec((1, HEAD_DIM, block), lambda i, *_: (0, 0, i))
    return pl.pallas_call(
        functools.partial(cross_forward_body, piece, real),
        grid_spec=pltpu.PrefetchScalarGridSpec(
            num_scalar_prefetch=2,
            grid=(width // block,),
            in_specs=[
                column,
                pl.BlockSpec((NSEG, 2, HEAD_DIM, span), lambda i, *_: (0, 0, 0, 0)),
                row,
            ],
            out_specs=[pl.BlockSpec((HEAD_DIM, block), lambda i, *_: (0, i)), column, row],
            scratch_shapes=[pltpu.VMEM((NSEG, span, HEAD_DIM), BF16)],
        ),
        out_shape=[
            jax.ShapeDtypeStruct((HEAD_DIM, width), F32),
            jax.ShapeDtypeStruct((1, HEAD_DIM, width), BF16),
            jax.ShapeDtypeStruct((1, width), F32),
        ],
        compiler_params=pltpu.CompilerParams(vmem_limit_bytes=VMEM_LIMIT),
    )(low, high, query, kv, qseg)


def cross_backward_body(piece, real, low_ref, high_ref, q_ref, kv_ref, qseg_ref, *rest):
    grad_ref, out_ref, log_ref, dq_ref, dkv_ref, key_ref, value_ref, acc_ref = rest
    step = pl.program_id(0)

    @pl.when(step == 0)
    def _():
        for slot in range(NSEG):
            key_ref[slot] = kv_ref[slot, 0].T
            value_ref[slot] = kv_ref[slot, 1].T
        acc_ref[...] = jnp.zeros_like(acc_ref)

    query, grad, segments, logs = q_ref[0], grad_ref[0], qseg_ref[...], log_ref[...]
    width, span = query.shape[1], kv_ref.shape[3]
    row_dot = jnp.sum(grad.astype(F32) * out_ref[...], axis=0, keepdims=True)
    present = page_rows(span, piece, real)

    def fold(slot, dq):
        scores = jnp.dot(key_ref[slot], query, preferred_element_type=F32)
        allowed = present & (segments == slot)
        weights = jnp.where(allowed, jnp.exp2(scores * EXP2_SCALE - logs), 0.0)
        weight_grad = jnp.dot(value_ref[slot], grad, preferred_element_type=F32)
        score_grad = (weights * (weight_grad - row_dot)).astype(BF16)
        acc_ref[slot, 1] += dot(grad, weights.astype(BF16), 1, 1)
        acc_ref[slot, 0] += dot(query, score_grad, 1, 1)
        return dq + jnp.dot(kv_ref[slot, 0], score_grad, preferred_element_type=F32)

    dq = jnp.zeros((HEAD_DIM, width), F32)
    dq = lax.fori_loop(low_ref[step], high_ref[step] + 1, fold, dq)
    dq_ref[0] = (dq * SCALE).astype(BF16)

    @pl.when(step == pl.num_programs(0) - 1)
    def _():
        for slot in range(NSEG):
            dkv_ref[slot, 0] = (acc_ref[slot, 0] * SCALE).astype(BF16)
            dkv_ref[slot, 1] = acc_ref[slot, 1].astype(BF16)


def cross_backward(query, kv, qseg, low, high, grad, out, log, piece, real):
    width, span = query.shape[2], kv.shape[3]
    block = min(512, width)
    row = pl.BlockSpec((1, block), lambda i, *_: (0, i))
    column = pl.BlockSpec((1, HEAD_DIM, block), lambda i, *_: (0, 0, i))
    pages = pl.BlockSpec((NSEG, 2, HEAD_DIM, span), lambda i, *_: (0, 0, 0, 0))
    return pl.pallas_call(
        functools.partial(cross_backward_body, piece, real),
        grid_spec=pltpu.PrefetchScalarGridSpec(
            num_scalar_prefetch=2,
            grid=(width // block,),
            in_specs=[
                column,
                pages,
                row,
                column,
                pl.BlockSpec((HEAD_DIM, block), lambda i, *_: (0, i)),
                row,
            ],
            out_specs=[column, pages],
            scratch_shapes=[
                pltpu.VMEM((NSEG, span, HEAD_DIM), BF16),
                pltpu.VMEM((NSEG, span, HEAD_DIM), BF16),
                pltpu.VMEM((NSEG, 2, HEAD_DIM, span), F32),
            ],
        ),
        out_shape=[
            jax.ShapeDtypeStruct((1, HEAD_DIM, width), BF16),
            jax.ShapeDtypeStruct((NSEG, 2, HEAD_DIM, span), BF16),
        ],
        compiler_params=pltpu.CompilerParams(vmem_limit_bytes=VMEM_LIMIT),
    )(low, high, query, kv, qseg, grad, out, log)


def layer_norm(value, gain):
    mean = jnp.mean(value, axis=-1, keepdims=True)
    centred = value - mean
    inv_std = lax.rsqrt(jnp.mean(centred * centred, axis=-1, keepdims=True) + EPS)
    unit = centred * inv_std
    return ((unit * gain).astype(BF16), unit, inv_std)


def norm_back(grad, unit, inv_std, gain):
    scaled = grad * gain
    inner = (
        scaled
        - jnp.mean(scaled, axis=-1, keepdims=True)
        - unit * jnp.mean(scaled * unit, axis=-1, keepdims=True)
    )
    return inner * inv_std


def other_core(value):
    return lax.ppermute(value, "tp", [(0, 1), (1, 0)])


def tp_total(partial_sum):
    low = partial_sum.astype(BF16)
    return low.astype(F32) + other_core(low).astype(F32)


def reduce_scatter(grad, count, place):
    bits = count.bit_length() - 1
    rows, columns = grad.shape[0] // count, grad.shape[1]
    grad = grad.reshape((2,) * bits + (rows, columns))

    def run(piece, order):
        left = list(range(bits - 1, -1, -1))
        for bit in order:
            axis = left.index(bit)
            left.remove(bit)
            mine = (place >> bit) & 1
            keep = lax.dynamic_index_in_dim(piece, mine, axis, keepdims=False)
            send = lax.dynamic_index_in_dim(piece, 1 - mine, axis, keepdims=False).astype(BF16)
            pairs = [(i, i ^ (1 << bit)) for i in range(count)]
            piece = keep.astype(F32) + lax.ppermute(send, "blk", pairs).astype(F32)
        return piece

    first = list(range(bits))
    second = [1, 0] + first[2:]
    half = columns // 2
    return jnp.concatenate([run(grad[..., :half], first), run(grad[..., half:], second)], axis=-1)


def local(
    tokens,
    memory,
    segment_ids,
    token_valid,
    segment_page,
    gain_one,
    weight_query,
    weight_key,
    weight_value,
    weight_out,
    gain_two,
    cross_query,
    cross_key,
    cross_value,
    cross_out,
    gain_three,
    weight_up,
    weight_down,
    cotangent,
):
    packs, rows, width = tokens.shape
    heads = weight_query.shape[1] // HEAD_DIM
    count, place = lax.axis_size("blk"), lax.axis_index("blk")
    lay = Layout(count, packs, heads, rows, memory.shape[0])
    parts, half = lay.parts, lay.half
    flat_rows, total = packs * rows, count * rows
    share = width // count
    pack, part = place // half, lax.rem(place, parts)

    residual_in = tokens.reshape(flat_rows, width).astype(F32)
    hidden_one, unit_one, inv_one = layer_norm(residual_in, gain_one)
    qkv_tokens = jnp.stack(
        [dot(w, hidden_one, 0, 1).astype(BF16) for w in (weight_query, weight_key, weight_value)]
    )
    memory_padded = jnp.pad(memory, ((0, lay.mem_pad - lay.mem_rows), (0, 0)))
    kv_memory = jnp.stack(
        [dot(w, memory_padded, 0, 1).astype(BF16) for w in (cross_key, cross_value)]
    )
    codes = jnp.broadcast_to((segment_ids * 2 + token_valid)[:, None, :], (packs, 8, rows))
    qkv, codes, kv_half = exchange(
        0, [lay.to_units(qkv_tokens), lay.codes_to_units(codes), lay.memory_to_units(kv_memory)]
    )
    codes = codes[:1]
    segments = codes >> 1
    key_codes = jnp.where((codes & 1) == 1, segments, -1).reshape(total, 1)

    def own_part(value):
        if parts == 1:
            return value
        split = value.reshape(value.shape[:-1] + (count // parts, parts, rows))
        split = lax.dynamic_index_in_dim(split, part, split.ndim - 2, keepdims=False)
        return split.reshape(value.shape[:-1] + (total // parts,))

    def all_parts(value):
        if parts == 1:
            return value
        split = value.reshape(value.shape[:-1] + (count // parts, 1, rows))
        split = jnp.broadcast_to(split, value.shape[:-1] + (count // parts, parts, rows))
        return split.reshape(value.shape[:-1] + (total,))

    def pick_part(value):
        return lax.dynamic_index_in_dim(value, part, 0, keepdims=False)

    query = own_part(qkv[:1]) if parts > 1 else qkv
    query_segments = own_part(segments)
    query_positions = own_part(jnp.arange(total, dtype=jnp.int32)[None])

    slot_pages = segment_page.reshape(packs, NSEG)
    pages_here = lay.pages_half
    kv_pages = (
        kv_half.reshape(pages_here, lay.pieces, 2, HEAD_DIM, lay.mem_pad)
        .transpose(0, 2, 3, 1, 4)
        .reshape(pages_here, 2, HEAD_DIM, lay.pieces * lay.mem_pad)
    )
    first_page = pack * pages_here
    own_pages = lax.dynamic_index_in_dim(slot_pages, pack, 0, keepdims=False)
    twin_pages = lax.dynamic_index_in_dim(slot_pages, 1 - pack, 0, keepdims=False)

    def pages_of(wanted):
        found = [
            lax.dynamic_index_in_dim(
                kv_pages, jnp.clip(wanted[s] - first_page, 0, pages_here - 1), 0, keepdims=False
            )
            for s in range(NSEG)
        ]
        return jnp.stack(found)

    def is_here(wanted):
        return (wanted >= first_page) & (wanted < first_page + pages_here)

    twin_pairs = [(i, (i + half) % count) for i in range(count)]
    kv_twin = lax.ppermute(pages_of(twin_pages), "blk", twin_pairs)
    kv_slots = jnp.where(is_here(own_pages)[:, None, None, None], pages_of(own_pages), kv_twin)

    attention, attention_low, attention_log = self_forward(
        query, qkv, key_codes, query_segments, query_positions, parts
    )
    (mixed,) = exchange(1, [lay.from_units(all_parts(attention_low))])
    mixed = pick_part(mixed)[0]
    residual_one = residual_in + tp_total(dot(mixed, weight_out, 0, 0))
    hidden_two, unit_two, inv_two = layer_norm(residual_one, gain_two)

    cross_tokens = dot(cross_query, hidden_two, 0, 1).astype(BF16)[None]
    (cross_unit,) = exchange(2, [lay.to_units(cross_tokens)])
    cross_unit = own_part(cross_unit)
    block = min(512, total // parts)
    blocks = query_segments.reshape(-1, block)
    low, high = blocks[:, 0], blocks[:, -1]
    cross_attention, cross_low, cross_log = cross_forward(
        cross_unit, kv_slots, query_segments, low, high, lay.mem_pad, lay.mem_rows
    )
    (cross_mixed,) = exchange(3, [lay.from_units(all_parts(cross_low))])
    cross_mixed = pick_part(cross_mixed)[0]
    residual_two = residual_one + tp_total(dot(cross_mixed, cross_out, 0, 0))
    hidden_three, unit_three, inv_three = layer_norm(residual_two, gain_three)

    up_value = dot(hidden_three, weight_up, 1, 0)
    gelu_value, gelu_back = jax.vjp(functools.partial(jax.nn.gelu, approximate=False), up_value)
    gelu_low = gelu_value.astype(BF16)
    result = residual_two + tp_total(dot(gelu_low, weight_down, 1, 0))
    out = result.astype(BF16).reshape(packs, rows, width)
    down_in = cotangent.reshape(flat_rows, width)
    up_grad = gelu_back(dot(down_in, weight_down, 1, 1))[0].astype(BF16)
    grad_hidden = tp_total(dot(up_grad, weight_up, 1, 1))
    grad_two = down_in.astype(F32) + norm_back(grad_hidden, unit_three, inv_three, gain_three)
    feed_share = reduce_scatter(
        jnp.concatenate([dot(down_in, gelu_low, 0, 0), dot(hidden_three, up_grad, 0, 0)], axis=1),
        count,
        place,
    )

    cross_in = grad_two.astype(BF16)
    cross_grad = dot(cross_out, cross_in, 1, 1).astype(BF16)[None]
    (cross_grad,) = exchange(4, [lay.to_units(cross_grad)])
    cross_dq, cross_dkv = cross_backward(
        cross_unit,
        kv_slots,
        query_segments,
        low,
        high,
        own_part(cross_grad),
        cross_attention,
        cross_log,
        lay.mem_pad,
        lay.mem_rows,
    )
    twin_dkv = lax.ppermute(cross_dkv, "blk", twin_pairs)
    page_ids = first_page + jnp.arange(pages_here, dtype=jnp.int32)
    page_grad = sum(
        jnp.where(
            (pages[s] == page_ids)[:, None, None, None], grads[s].astype(F32)[None], 0.0
        )
        for pages, grads in ((own_pages, cross_dkv), (twin_pages, twin_dkv))
        for s in range(NSEG)
    ).astype(BF16)
    page_grad = (
        page_grad.reshape(pages_here, 2, HEAD_DIM, lay.pieces, lay.mem_pad)
        .transpose(0, 3, 1, 2, 4)
        .reshape(half, 2, HEAD_DIM, lay.mem_pad)
    )
    cross_dq_tokens, memory_grad = exchange(
        5, [lay.from_units(all_parts(cross_dq)), lay.memory_from_units(page_grad)]
    )
    cross_dq = pick_part(cross_dq_tokens)[0]
    if parts > 1:
        memory_grad = jnp.sum(memory_grad.astype(F32), axis=0).astype(BF16)
    else:
        memory_grad = memory_grad[0]
    dkc, dvc = memory_grad[0], memory_grad[1]
    grad_memory = tp_total(dot(dkc, cross_key, 0, 1) + dot(dvc, cross_value, 0, 1))
    grad_memory = grad_memory[: lay.mem_rows]

    grad_hidden = tp_total(dot(cross_dq, cross_query, 0, 1))
    grad_one = grad_two + norm_back(grad_hidden, unit_two, inv_two, gain_two)

    self_in = grad_one.astype(BF16)
    mixed_grad = dot(weight_out, self_in, 1, 1).astype(BF16)[None]
    (mixed_grad,) = exchange(6, [lay.to_units(mixed_grad)])
    middle_share = reduce_scatter(
        jnp.concatenate(
            [
                dot(cross_in, cross_mixed, 0, 1),
                dot(hidden_two, cross_dq, 0, 1),
                dot(memory_padded, dkc, 0, 1),
                dot(memory_padded, dvc, 0, 1),
                dot(self_in, mixed, 0, 1),
            ],
            axis=1,
        ),
        count,
        place,
    )
    dq, dkv = self_backward(
        query,
        qkv,
        key_codes,
        query_segments,
        query_positions,
        own_part(mixed_grad),
        attention,
        attention_log,
        parts,
    )
    (dqkv,) = exchange(7, [lay.from_units(jnp.concatenate([all_parts(dq), dkv], axis=0))])
    if parts > 1:
        dkv = jnp.sum(dqkv[:, 1:].astype(F32), axis=0).astype(BF16)
        dq, dk, dv = pick_part(dqkv)[0], dkv[0], dkv[1]
    else:
        dq, dk, dv = dqkv[0, 0], dqkv[0, 1], dqkv[0, 2]
    grad_hidden = tp_total(
        dot(dq, weight_query, 0, 1) + dot(dk, weight_key, 0, 1) + dot(dv, weight_value, 0, 1)
    )
    grad_input = grad_one + norm_back(grad_hidden, unit_one, inv_one, gain_one)
    grad_input = grad_input.reshape(packs, rows, width)
    first_share = reduce_scatter(
        jnp.concatenate([dot(hidden_one, d, 0, 1) for d in (dq, dk, dv)], axis=1), count, place
    )

    ff, wide = weight_up.shape[1], weight_query.shape[1]
    grad_down, grad_up = feed_share[:, :ff].T, feed_share[:, ff:]
    middle = [middle_share[:, i * wide : (i + 1) * wide] for i in range(5)]
    first = [first_share[:, i * wide : (i + 1) * wide] for i in range(3)]

    def own_rows(weight):
        return lax.dynamic_slice_in_dim(weight, place * share, share, 0).astype(F32)

    sums = jnp.stack(
        [
            sum(
                jnp.sum(own_rows(w) * g, axis=1)
                for w, g in zip((weight_query, weight_key, weight_value), first, strict=True)
            ),
            jnp.sum(own_rows(cross_query) * middle[1], axis=1),
            jnp.sum(own_rows(weight_up) * grad_up, axis=1),
        ]
    )
    gains = jnp.stack(
        [lax.dynamic_slice_in_dim(g, place * share, share) for g in (gain_one, gain_two, gain_three)]
    )
    gain_grads = (sums + other_core(sums)) / gains
    return (
        out,
        grad_input,
        grad_memory,
        first[0],
        first[1],
        first[2],
        middle[4].T,
        middle[1],
        middle[2],
        middle[3],
        middle[0].T,
        grad_up,
        grad_down,
        gain_grads[0],
        gain_grads[1],
        gain_grads[2],
    )


def solution(mesh):
    in_specs = (
        P(None, "blk", None),
        P("blk", None),
        P(None, "blk"),
        P(None, "blk"),
        P(),
        P(),
        P(None, "tp"),
        P(None, "tp"),
        P(None, "tp"),
        P("tp", None),
        P(),
        P(None, "tp"),
        P(None, "tp"),
        P(None, "tp"),
        P("tp", None),
        P(),
        P(None, "tp"),
        P("tp", None),
        P(None, "blk", None),
    )
    out_specs = (
        P(None, "blk", None),
        P(None, "blk", None),
        P("blk", None),
        P("blk", "tp"),
        P("blk", "tp"),
        P("blk", "tp"),
        P("tp", "blk"),
        P("blk", "tp"),
        P("blk", "tp"),
        P("blk", "tp"),
        P("tp", "blk"),
        P("blk", "tp"),
        P("tp", "blk"),
        P("blk"),
        P("blk"),
        P("blk"),
    )
    return jax.shard_map(local, mesh=mesh, in_specs=in_specs, out_specs=out_specs, check_vma=False)
```

time: 4700 us -> 592 us (0.13)
  blocking collectives: 1730 us -> 0 us
  waiting for transfers between devices: 1710 us -> 139 us
  local copies, waits for them, and re-layouts: 871 us -> 79.6 us
  Pallas kernels: 0 us -> 217 us
  matrix products: 215 us -> 45.4 us
    unnamed x1 -> x0, blocking collectives: 1650 us -> none
    reduce_scatter x12 -> x0, waiting for transfers between devices: 1080 us -> none  [the longest x2 189 us: local(): lax.psum_scatter(value_terms.reshape(total_rows, local_width), 'blk', sca...]
    dynamic_update_slice x64 -> x0, local copies, waits for them, and re-layouts: 665 us -> none  [the longest x48 488 us: cross_backward(): lax.scan(page_step, start_grad, (page_keys, page_values, pages))]
    all_gather x8 -> x0, waiting for transfers between devices: 410 us -> none  [the longest x1 123 us: local(): lax.all_gather(own_keys, 'blk', axis=0, tiled=True)]
    pallas_call x0 -> x12, Pallas kernels: none -> 217 us  [the longest x8 178 us: exchange(): pl.pallas_call(body, out_shape=[jax.ShapeDtypeStruct(item[1], item[0].dty...]
    dot_general x100 -> x30, matrix products: 215 us -> 45.4 us  [dot(): lax.dot_general(left, right, (((contract_left,), (contract_right,)), ((),...]
    unnamed x30 -> x0, waiting for transfers between devices: 163 us -> none
    ppermute x0 -> x34, waiting for transfers between devices: none -> 139 us  [the longest x24 119 us: run(): piece = keep.astype(F32) + lax.ppermute(send, 'blk', pairs).astype(F32)]
  transfers between devices with their start and end apart: 28 -> 34, of which waited for: 22 -> 14; matrix products, arithmetic and copies ran while one was open for 10% -> 25% of each run, Pallas kernels for 0% -> 25%
where the time goes in v1:
time: 592 us; the launch traced here: 585 us
  Pallas kernels  217 us (37%)
  waiting for transfers between devices  139 us (23%)
  local copies, waits for them, and re-layouts  79.6 us (13%)
  other arithmetic  67.6 us (11%)
  matrix products  45.4 us (8%)
  starting transfers between devices  30.5 us (5%)
  between operations  5.96 us (1%)
    pallas_call x8, Pallas kernels, exchange(): pl.pallas_call(body, out_shape=[jax.ShapeDtypeStruct(item[1], item[0].dty...  178 us
    ppermute x24, waiting for transfers between devices, run(): piece = keep.astype(F32) + lax.ppermute(send, 'blk', pairs).astype(F32)  119 us
    dot_general x30, matrix products, dot(): lax.dot_general(left, right, (((contract_left,), (contract_right,)), ((),...  45.4 us
    ppermute x24, starting transfers between devices, run(): piece = keep.astype(F32) + lax.ppermute(send, 'blk', pairs).astype(F32)  28 us
    ppermute x1, waiting for transfers between devices, local(): twin_dkv = lax.ppermute(cross_dkv, 'blk', twin_pairs)  19.8 us
    concatenate x1, local copies, waits for them, and re-layouts, local(): jnp.concatenate([dot(down_in, gelu_low, 0, 0), dot(hidden_three, up_grad,...  17.5 us
    add x22, other arithmetic, run(): piece = keep.astype(F32) + lax.ppermute(send, 'blk', pairs).astype(F32)  13.6 us
  transfers between devices with their start and end apart: 34, of which 14 were waited for; matrix products, arithmetic and copies ran while one was open for 25% of the time, Pallas kernels for 25%

profile of v1, /device:TPU:0, one launch (start us, length us, event | category | flops | bytes accessed | tf_op | source)
XLA Modules:
  0.0 585.2 jit_solution(15661189206770164053)
XLA Ops:
  8.1 1.9 fusion.13
  15.2 2.3 pad_maximum_fusion.2.refs_2_
  19.0 39.3 %shard_map.306 = (bf16[3,64,2048]{2,1,0:T(8,128)(2,1)}, s32[8,2048]{1,0:T(8,128)}, bf16[8,2,64,640]{3,2,1,0:T(8,128)(2,1)}) custom-call(bf16[3,512,256]{2,1,0:T(8,128)(2,1)} %pad_maximum_fusion.3.refs_0_, s32[2,8,128]{2,1,0:T(8,128)} %broadcast_in_dim.164.refs_1_, bf16[2,512,640]{2,1,0:T(8,128)(2,1)} %pad_maximum_fusion.2.refs_2_), custom_call_target="tpu_custom_call" | custom-call | tf_op jit(solution)/shard_map/pallas_call | solution.py:69
  58.4 2.1 constant_dynamic-slice_fusion.10
  64.7 9.3 %shard_map.307 = (f32[64,2048]{1,0:T(8,128)}, bf16[1,64,2048]{2,1,0:T(8,128)(2,1)}, f32[1,2048]{1,0:T(1,128)}) custom-call(bf16[3,64,2048]{2,1,0:T(8,128)(2,1)} %get-tuple-element.31.q_ref.k_ref.v_ref, bf16[3,64,2048]{2,1,0:T(8,128)(2,1)} %get-tuple-element.31.q_ref.k_ref.v_ref, bf16[3,64,2048]{2,1,0:T(8,128)(2,1)} %get-tuple-element.31.q_ref.k_ref.v_ref, ...), custom_call_target="tpu_custom_call" | custom-call | tf_op jit(solution)/shard_map/pallas_call | solution.py:206
  74.1 17.8 %shard_map.308 = bf16[1,1,512,256]{3,2,1,0:T(8,128)(2,1)} custom-call(bf16[1,64,2048]{2,1,0:T(8,128)(2,1)} %get-tuple-element.33.refs_0_), custom_call_target="tpu_custom_call" | custom-call | tf_op jit(solution)/shard_map/pallas_call | solution.py:69
  97.2 2.0 maximum_select_fusion.kv_ref
  102.3 11.6 %shard_map.309.q_ref = bf16[1,64,2048]{2,1,0:T(8,128)(2,1)} custom-call(bf16[1,512,256]{2,1,0:T(8,128)(2,1)} %fusion.18.refs_0_), custom_call_target="tpu_custom_call" | custom-call | tf_op jit(solution)/shard_map/pallas_call | solution.py:69
  113.9 7.7 %shard_map.310 = (f32[64,2048]{1,0:T(8,128)}, bf16[1,64,2048]{2,1,0:T(8,128)(2,1)}, f32[1,2048]{1,0:T(1,128)}) custom-call(s32[4]{0:T(128)} %bitcast.315, s32[4]{0:T(128)} %bitcast.317, bf16[1,64,2048]{2,1,0:T(8,128)(2,1)} %shard_map.309.q_ref, bf16[3,2,64,640]{3,2,1,0:T(8,128)(2,1)} %maximum_select_fusion.kv_ref, s32[1,2048]{1,0:T(1,128)} %get-tuple-element.101.qseg_ref), custom_call_target="tpu_custom_call" | custom-call | tf_op jit(solution)/shard_map/pallas_call | solution.py:353
  121.6 10.6 %shard_map.311 = bf16[1,1,512,256]{3,2,1,0:T(8,128)(2,1)} custom-call(bf16[1,64,2048]{2,1,0:T(8,128)(2,1)} %get-tuple-element.35.refs_0_), custom_call_target="tpu_custom_call" | custom-call | tf_op jit(solution)/shard_map/pallas_call | solution.py:69
  132.2 1.8 convolution_convert_fusion.3
  141.6 6.8 %add_convert_fusion.2 = (bf16[256,2048]{1,0:T(8,128)(2,1)S(1)}, f32[256,2048]{1,0:T(8,128)S(1)}) fusion(f32[256,2048]{1,0:T(8,128)S(1)} %fusion.116, bf16[256,1024]{1,0:T(8,128)(2,1)S(1)} %bitcast.309, bf16[2048,1024]{1,0:T(8,128)(2,1)S(1)} %copy-done.41), kind=kOutput, calls=%fused_computation.23 | convolution fusion | flops 1111490560 | bytes 9961472 | tf_op jit(solution)/shard_map/dot_general | solution.py:25
  148.4 2.1 convolution_convert_fusion.5
  152.2 2.1 convolution_convert_fusion.6
  156.3 6.4 %pad_maximum_fusion = f32[1024,4096]{0,1:T(8,128)} fusion(f32[1024,2048]{0,1:T(8,128)S(1)} %fusion.115, f32[1024,2048]{0,1:T(8,128)S(1)} %convolution_bitcast_fusion), kind=kLoop, calls=%fused_computation | loop fusion | flops 4194304 | bytes 33554432 | tf_op jit(solution)/shard_map/concatenate | solution.py:623
  162.7 17.5 %copy.69 = f32[1024,4096]{1,0:T(8,128)} copy(f32[1024,4096]{0,1:T(8,128)} %pad_maximum_fusion) | data formatting | bytes 33554432 | tf_op jit(solution)/shard_map/concatenate | solution.py:623
  180.2 6.5 %fusion.120 = (f32[2,2,2,2,64,2048]{5,4,3,2,1,0:T(8,128)S(1)}, f32[2,2,2,2,64,2048]{5,4,3,2,1,0:T(8,128)S(1)}) fusion(f32[2,2,2,2,64,4096]{5,4,3,2,1,0:T(8,128)} %bitcast.301), kind=kLoop, calls=%fused_computation.281 | loop fusion | bytes 33554432 | tf_op jit(solution)/shard_map/slice | solution.py:493
  186.7 1.9 fusion.2
  189.1 2.4 fusion.3
  192.5 2.4 fusion.41
  194.9 2.9 multiply_add_fusion.1
  199.9 43.6 %shard_map.312.rest_0_ = bf16[1,64,2048]{2,1,0:T(8,128)(2,1)} custom-call(bf16[1,512,256]{2,1,0:T(8,128)(2,1)} %fusion.19.refs_0_), custom_call_target="tpu_custom_call" | custom-call | tf_op jit(solution)/shard_map/pallas_call | solution.py:69
  243.5 10.4 %shard_map.313 = (bf16[1,64,2048]{2,1,0:T(8,128)(2,1)}, bf16[3,2,64,640]{3,2,1,0:T(8,128)(2,1)}) custom-call(s32[4]{0:T(128)} %bitcast.316, s32[4]{0:T(128)} %bitcast.318, bf16[1,64,2048]{2,1,0:T(8,128)(2,1)} %shard_map.309.q_ref, bf16[3,2,64,640]{3,2,1,0:T(8,128)(2,1)} %maximum_select_fusion.kv_ref, s32[1,2048]{1,0:T(1,128)} %get-tuple-element.101.qseg_ref, ...), custom_call_target="tpu_custom_call" | custom-call | tf_op jit(solution)/shard_map/pallas_call | solution.py:418
  256.2 1.8 convolution_dynamic-update-slice_fusion.4
  258.0 19.8 %collective-permute-done.5 = bf16[3,2,64,640]{3,2,1,0:T(8,128)(2,1)S(1)} collective-permute-done((bf16[3,2,64,640]{3,2,1,0:T(8,128)(2,1)}, bf16[3,2,64,640]{3,2,1,0:T(8,128)(2,1)S(1)}, u32[]{:S(2)}, u32[]{:S(2)}) %collective-permute-start.5) | collective-permute-done | bytes 491552 | tf_op jit(solution)/shard_map/ppermute | solution.py:643
  277.8 2.6 add_convert_fusion.1.refs_1_
  280.5 24.7 %shard_map.314 = (bf16[1,1,512,256]{3,2,1,0:T(8,128)(2,1)}, bf16[1,2,512,640]{3,2,1,0:T(8,128)(2,1)}) custom-call(bf16[1,64,2048]{2,1,0:T(8,128)(2,1)} %get-tuple-element.38.refs_0_, bf16[8,2,64,640]{3,2,1,0:T(8,128)(2,1)} %add_convert_fusion.1.refs_1_), custom_call_target="tpu_custom_call" | custom-call | tf_op jit(solution)/shard_map/pallas_call | solution.py:69
  305.2 1.9 convolution_convert_fusion.2
  308.5 2.0 add_convert_fusion
  310.9 1.9 convolution_dynamic-update-slice_fusion.3
  312.9 2.4 convolution_dynamic-update-slice_fusion.2
  315.2 2.4 convolution_dynamic-update-slice_fusion.1
  320.5 11.1 %shard_map.315.rest_0_ = bf16[1,64,2048]{2,1,0:T(8,128)(2,1)} custom-call(bf16[1,512,256]{2,1,0:T(8,128)(2,1)} %fusion.20.refs_0_), custom_call_target="tpu_custom_call" | custom-call | tf_op jit(solution)/shard_map/pallas_call | solution.py:69
  332.2 11.6 %shard_map.316 = (bf16[1,64,2048]{2,1,0:T(8,128)(2,1)}, bf16[2,64,2048]{2,1,0:T(8,128)(2,1)}) custom-call(bf16[3,64,2048]{2,1,0:T(8,128)(2,1)} %get-tuple-element.31.q_ref.k_ref.v_ref, bf16[3,64,2048]{2,1,0:T(8,128)(2,1)} %get-tuple-element.31.q_ref.k_ref.v_ref, bf16[3,64,2048]{2,1,0:T(8,128)(2,1)} %get-tuple-element.31.q_ref.k_ref.v_ref, ...), custom_call_target="tpu_custom_call" | custom-call | tf_op jit(solution)/shard_map/pallas_call | solution.py:280
  343.8 2.1 pad_maximum_fusion.4.refs_0_
  345.9 19.6 %shard_map.317 = bf16[1,3,512,256]{3,2,1,0:T(8,128)(2,1)} custom-call(bf16[3,64,2048]{2,1,0:T(8,128)(2,1)} %pad_maximum_fusion.4.refs_0_), custom_call_target="tpu_custom_call" | custom-call | tf_op jit(solution)/shard_map/pallas_call | solution.py:69
  371.0 3.2 pad_maximum_fusion.1
  374.2 6.5 %copy.64 = f32[1024,1536]{1,0:T(8,128)} copy(f32[1024,1536]{0,1:T(8,128)} %pad_maximum_fusion.1) | data formatting | bytes 12582912 | tf_op jit(solution)/shard_map/concatenate | solution.py:712
  380.8 5.2 fusion.122
  389.2 1.8 convolution_dynamic-update-slice_fusion
  390.9 11.5 %copy.66 = f32[1024,2560]{1,0:T(8,128)} copy(f32[1024,2560]{0,1:T(8,128)} %convolution_dynamic-update-slice_fusion) | data formatting | bytes 20971520 | tf_op jit(solution)/shard_map/concatenate | solution.py:676
  402.4 4.9 fusion.121
  407.4 2.4 fusion.45
  416.2 3.7 bitcast_add_fusion.1
  421.4 2.5 bitcast_add_fusion
  427.2 5.7 collective-permute-done.9
  436.9 3.5 convert_add_fusion
  440.4 50.6 %collective-permute-done.14 = bf16[2,2,64,768]{3,2,1,0:T(8,128)(2,1)S(1)} collective-permute-done((bf16[2,2,64,768]{3,2,1,0:T(8,128)(2,1)S(1)}, bf16[2,2,64,768]{3,2,1,0:T(8,128)(2,1)S(1)}, u32[]{:S(2)}, u32[]{:S(2)}) %collective-permute-start.14) | collective-permute-done | bytes 393248 | tf_op jit(solution)/shard_map/ppermute | solution.py:487
  492.7 2.7 collective-permute-start.15
  503.8 2.2 collective-permute-start.16
  506.0 3.2 collective-permute-done.16
  509.3 2.2 collective-permute-start.12
  511.5 3.3 collective-permute-done.12
  514.8 1.8 multiply_reduce_fusion.6
  517.0 1.8 collective-permute-start.27
  520.3 9.3 %collective-permute-done.22 = bf16[2,2,64,1280]{3,2,1,0:T(8,128)(2,1)S(1)} collective-permute-done((bf16[2,2,64,1280]{3,2,1,0:T(8,128)(2,1)S(1)}, bf16[2,2,64,1280]{3,2,1,0:T(8,128)(2,1)S(1)}, u32[]{:S(2)}, u32[]{:S(2)}) %collective-permute-start.22) | collective-permute-done | bytes 655392 | tf_op jit(solution)/shard_map/ppermute | solution.py:487
  529.8 2.7 collective-permute-start.23
  533.0 2.5 collective-permute-start.28
  535.5 16.1 %collective-permute-done.31 = bf16[2,64,2048]{2,1,0:T(8,128)(2,1)S(1)} collective-permute-done((bf16[2,64,2048]{2,1,0:T(8,128)(2,1)S(1)}, bf16[2,64,2048]{2,1,0:T(8,128)(2,1)S(1)}, u32[]{:S(2)}, u32[]{:S(2)}) %collective-permute-start.31) | collective-permute-done | bytes 524320 | tf_op jit(solution)/shard_map/ppermute | solution.py:487
  551.8 8.2 %collective-permute-done.23 = bf16[2,64,1280]{2,1,0:T(8,128)(2,1)S(1)} collective-permute-done((bf16[2,64,1280]{2,1,0:T(8,128)(2,1)S(1)}, bf16[2,64,1280]{2,1,0:T(8,128)(2,1)S(1)}, u32[]{:S(2)}, u32[]{:S(2)}) %collective-permute-start.23) | collective-permute-done | bytes 327712 | tf_op jit(solution)/shard_map/ppermute | solution.py:487
  560.2 4.0 collective-permute-done.19
  564.4 1.9 multiply_reduce_fusion.4
  566.4 13.3 %collective-permute-done.24 = bf16[64,1280]{1,0:T(8,128)(2,1)S(1)} collective-permute-done((bf16[64,1280]{1,0:T(8,128)(2,1)S(1)}, bf16[64,1280]{1,0:T(8,128)(2,1)S(1)}, u32[]{:S(2)}, u32[]{:S(2)}) %collective-permute-start.24) | collective-permute-done | bytes 163872 | tf_op jit(solution)/shard_map/ppermute | solution.py:487
  581.4 1.8 slice_bitcast_fusion.3
  (256 shorter events, 85.3 us)
Async XLA Ops:
  0.6 7.4 %copy-start = (bf16[1024,512]{1,0:T(8,128)(2,1)S(1)}, bf16[1024,512]{1,0:T(8,128)(2,1)}, u32[]{:S(2)}) copy-start(bf16[1024,512]{1,0:T(8,128)(2,1)} %param.31) | copy-start | bytes 3145732
  0.7 4.1 copy-start.20
  0.7 4.6 copy-start.15
  8.1 7.1 %copy-start.38 = (s32[2,128]{1,0:T(2,128)S(1)}, s32[2,128]{1,0:T(2,128)}, u32[]{:S(2)}) copy-start(s32[2,128]{1,0:T(2,128)} %param.22) | copy-start | bytes 3076
  8.1 7.1 %copy-start.39 = (s32[2,128]{1,0:T(2,128)S(1)}, s32[2,128]{1,0:T(2,128)}, u32[]{:S(2)}) copy-start(s32[2,128]{1,0:T(2,128)} %param.21) | copy-start | bytes 3076
  61.3 35.9 %collective-permute-start.1 = (bf16[3,2,64,640]{3,2,1,0:T(8,128)(2,1)}, bf16[3,2,64,640]{3,2,1,0:T(8,128)(2,1)}, u32[]{:S(2)}, u32[]{:S(2)}) collective-permute-start(bf16[3,2,64,640]{3,2,1,0:T(8,128)(2,1)} %pad_maximum_fusion.5), channel_id=1, source_target_pairs={{0,16},{2,18},{4,20},{6,22},{8,24},{10,26},{12,28},{14,30},{16,0},... | collective-permute-start | bytes 1474568 | tf_op jit(solution)/shard_map/ppermute | solution.py:588
  64.1 27.7 %copy-start.23 = (bf16[512,1024]{1,0:T(8,128)(2,1)S(1)}, bf16[512,1024]{1,0:T(8,128)(2,1)}, u32[]{:S(2)}) copy-start(bf16[512,1024]{1,0:T(8,128)(2,1)} %param.28) | copy-start | bytes 3145732
  74.1 25.2 %copy-start.2 = (bf16[2,128,1024]{2,1,0:T(8,128)(2,1)S(1)}, bf16[2,128,1024]{2,1,0:T(8,128)(2,1)}, u32[]{:S(2)}) copy-start(bf16[2,128,1024]{2,1,0:T(8,128)(2,1)} %param.19) | copy-start | bytes 1572868
  93.3 6.0 %collective-permute-start = (bf16[256,1024]{1,0:T(8,128)(2,1)S(1)}, bf16[256,1024]{1,0:T(8,128)(2,1)}, u32[]{:S(2)}, u32[]{:S(2)}) collective-permute-start(bf16[256,1024]{1,0:T(8,128)(2,1)S(1)} %convolution_convert_fusion.4), channel_id=1, source_target_pairs={{0,1},{1,0},{2,3},{3,2},{4,5},{5,4},{6,7},{7,6},{8,9},{9,8},{10,11... | collective-permute-start | bytes 1572872 | tf_op jit(solution)/shard_map/ppermute | solution.py:465
  102.3 31.8 %copy-start.34 = (f32[1024]{0:T(1024)S(1)}, f32[1024]{0:T(1024)}, u32[]{:S(2)}) copy-start(f32[1024]{0:T(1024)} %param.34) | copy-start | bytes 12292
  102.3 33.2 %copy-start.35 = (f32[1024]{0:T(1024)S(1)}, f32[1024]{0:T(1024)}, u32[]{:S(2)}) copy-start(f32[1024]{0:T(1024)} %param.24) | copy-start | bytes 12292
  134.0 2.7 copy-start.29
  134.0 2.7 collective-permute-start.2
  136.7 2.5 copy-start.37
  139.2 2.4 copy-start.41
  155.7 36.8 %collective-permute-start.4 = (bf16[256,1024]{1,0:T(8,128)(2,1)}, bf16[256,1024]{1,0:T(8,128)(2,1)}, u32[]{:S(2)}, u32[]{:S(2)}) collective-permute-start(bf16[256,1024]{1,0:T(8,128)(2,1)} %convolution_convert_fusion.5), channel_id=1, source_target_pairs={{0,1},{1,0},{2,3},{3,2},{4,5},{5,4},{6,7},{7,6},{8,9},{9,8},{10,11... | collective-permute-start | bytes 1572872 | tf_op jit(solution)/shard_map/ppermute | solution.py:465
  156.2 38.6 %collective-permute-start.3 = (bf16[256,1024]{1,0:T(8,128)(2,1)}, bf16[256,1024]{1,0:T(8,128)(2,1)}, u32[]{:S(2)}, u32[]{:S(2)}) collective-permute-start(bf16[256,1024]{1,0:T(8,128)(2,1)} %convolution_convert_fusion.6), channel_id=1, source_target_pairs={{0,1},{1,0},{2,3},{3,2},{4,5},{5,4},{6,7},{7,6},{8,9},{9,8},{10,11... | collective-permute-start | bytes 1572872 | tf_op jit(solution)/shard_map/ppermute | solution.py:465
  186.7 11.1 %copy-start.4 = (f32[2,2,2,2,64,2048]{5,4,3,2,1,0:T(8,128)}, f32[2,2,2,2,64,2048]{5,4,3,2,1,0:T(8,128)S(1)}, u32[]{:S(2)}) copy-start(f32[2,2,2,2,64,2048]{5,4,3,2,1,0:T(8,128)S(1)} %get-tuple-element.70) | copy-start | bytes 25165828
  186.7 11.1 %copy-start.5 = (f32[2,2,2,2,64,2048]{5,4,3,2,1,0:T(8,128)}, f32[2,2,2,2,64,2048]{5,4,3,2,1,0:T(8,128)S(1)}, u32[]{:S(2)}) copy-start(f32[2,2,2,2,64,2048]{5,4,3,2,1,0:T(8,128)S(1)} %get-tuple-element.71) | copy-start | bytes 25165828
  188.6 226.6 %collective-permute-start.25 = (bf16[2,2,2,64,2048]{4,3,2,1,0:T(8,128)(2,1)}, bf16[2,2,2,64,2048]{4,3,2,1,0:T(8,128)(2,1)}, u32[]{:S(2)}, u32[]{:S(2)}) collective-permute-start(bf16[2,2,2,64,2048]{4,3,2,1,0:T(8,128)(2,1)} %fusion.2), channel_id=1, source_target_pairs={{0,4},{2,6},{4,0},{6,2},{8,12},{10,14},{12,8},{14,10},{16,20},{18,... | collective-permute-start | bytes 6291464 | tf_op jit(solution)/shard_map/ppermute | solution.py:487
  191.5 3.3 copy-start.28
  191.5 228.4 %collective-permute-start.29 = (bf16[2,2,2,64,2048]{4,3,2,1,0:T(8,128)(2,1)}, bf16[2,2,2,64,2048]{4,3,2,1,0:T(8,128)(2,1)}, u32[]{:S(2)}, u32[]{:S(2)}) collective-permute-start(bf16[2,2,2,64,2048]{4,3,2,1,0:T(8,128)(2,1)} %fusion.3), channel_id=1, source_target_pairs={{0,2},{2,0},{4,6},{6,4},{8,10},{10,8},{12,14},{14,12},{16,18},{18,... | collective-permute-start | bytes 6291464 | tf_op jit(solution)/shard_map/ppermute | solution.py:487
  194.9 3.8 copy-start.22
  199.9 56.3 %copy-start.7 = (f32[256,1024]{1,0:T(8,128)S(1)}, f32[256,1024]{1,0:T(8,128)}, u32[]{:S(2)}) copy-start(f32[256,1024]{1,0:T(8,128)} %copy-done.6) | copy-start | bytes 3145732
  199.9 56.3 %copy-start.26 = (bf16[1,1,512,256]{3,2,1,0:T(8,128)(2,1)S(1)}, bf16[1,1,512,256]{3,2,1,0:T(8,128)(2,1)}, u32[]{:S(2)}) copy-start(bf16[1,1,512,256]{3,2,1,0:T(8,128)(2,1)} %shard_map.311) | copy-start | bytes 786436
  254.0 23.8 %collective-permute-start.5 = (bf16[3,2,64,640]{3,2,1,0:T(8,128)(2,1)}, bf16[3,2,64,640]{3,2,1,0:T(8,128)(2,1)S(1)}, u32[]{:S(2)}, u32[]{:S(2)}) collective-permute-start(bf16[3,2,64,640]{3,2,1,0:T(8,128)(2,1)} %get-tuple-element.39), channel_id=1, source_target_pairs={{0,16},{2,18},{4,20},{6,22},{8,24},{10,26},{12,28},{14,30},{16,0},... | collective-permute-start | bytes 1474568 | tf_op jit(solution)/shard_map/ppermute | solution.py:643
  307.1 10.5 %collective-permute-start.6 = (bf16[256,1024]{1,0:T(8,128)(2,1)S(1)}, bf16[256,1024]{1,0:T(8,128)(2,1)S(1)}, u32[]{:S(2)}, u32[]{:S(2)}) collective-permute-start(bf16[256,1024]{1,0:T(8,128)(2,1)S(1)} %convolution_convert_fusion.2), channel_id=1, source_target_pairs={{0,1},{1,0},{2,3},{3,2},{4,5},{5,4},{6,7},{7,6},{8,9},{9,8},{10,11... | collective-permute-start | bytes 1572872 | tf_op jit(solution)/shard_map/ppermute | solution.py:465
  308.5 2.5 copy-start.31
  310.4 2.4 copy-start.43
  310.4 124.9 %collective-permute-start.8 = (bf16[640,1024]{1,0:T(8,128)(2,1)}, bf16[640,1024]{1,0:T(8,128)(2,1)}, u32[]{:S(2)}, u32[]{:S(2)}) collective-permute-start(bf16[640,1024]{1,0:T(8,128)(2,1)} %add_convert_fusion), channel_id=1, source_target_pairs={{0,1},{1,0},{2,3},{3,2},{4,5},{5,4},{6,7},{7,6},{8,9},{9,8},{10,11... | collective-permute-start | bytes 3932168 | tf_op jit(solution)/shard_map/ppermute | solution.py:465
  319.3 69.9 %copy-start.8 = (f32[256,1024]{1,0:T(8,128)}, f32[256,1024]{1,0:T(8,128)S(1)}, u32[]{:S(2)}) copy-start(f32[256,1024]{1,0:T(8,128)S(1)} %multiply_add_fusion) | copy-start | bytes 3145732
  343.8 21.8 %copy-start.18 = (bf16[1024,512]{1,0:T(8,128)(2,1)S(1)}, bf16[1024,512]{1,0:T(8,128)(2,1)}, u32[]{:S(2)}) copy-start(bf16[1024,512]{1,0:T(8,128)(2,1)} %param.25) | copy-start | bytes 3145732
  345.9 21.1 %copy-start.13 = (bf16[2,128,1024]{2,1,0:T(8,128)(2,1)S(1)}, bf16[2,128,1024]{2,1,0:T(8,128)(2,1)}, u32[]{:S(2)}) copy-start(bf16[2,128,1024]{2,1,0:T(8,128)(2,1)} %fusion.27) | copy-start | bytes 1572868
  371.0 41.3 %collective-permute-start.7 = (bf16[256,1024]{1,0:T(8,128)(2,1)S(1)}, bf16[256,1024]{1,0:T(8,128)(2,1)S(1)}, u32[]{:S(2)}, u32[]{:S(2)}) collective-permute-start(bf16[256,1024]{1,0:T(8,128)(2,1)S(1)} %fusion.12), channel_id=1, source_target_pairs={{0,1},{1,0},{2,3},{3,2},{4,5},{5,4},{6,7},{7,6},{8,9},{9,8},{10,11... | collective-permute-start | bytes 1572872 | tf_op jit(solution)/shard_map/ppermute | solution.py:465
  380.8 8.4 %copy-start.25 = (bf16[1,1,512,256]{3,2,1,0:T(8,128)(2,1)S(1)}, bf16[1,1,512,256]{3,2,1,0:T(8,128)(2,1)}, u32[]{:S(2)}) copy-start(bf16[1,1,512,256]{3,2,1,0:T(8,128)(2,1)} %shard_map.308) | copy-start | bytes 786436
  388.6 35.7 %collective-permute-start.13 = (bf16[2,2,2,64,768]{4,3,2,1,0:T(8,128)(2,1)}, bf16[2,2,2,64,768]{4,3,2,1,0:T(8,128)(2,1)}, u32[]{:S(2)}, u32[]{:S(2)}) collective-permute-start(bf16[2,2,2,64,768]{4,3,2,1,0:T(8,128)(2,1)} %fusion.44), channel_id=1, source_target_pairs={{0,4},{2,6},{4,0},{6,2},{8,12},{10,14},{12,8},{14,10},{16,20},{18,... | collective-permute-start | bytes 2359304 | tf_op jit(solution)/shard_map/ppermute | solution.py:487
  409.8 3.5 copy-start.3
  411.0 2.7 copy-start.9
  411.0 10.4 %slice-start = ((s8[8388608]{0:T(1024)(128)(4,1)}), s8[4194304]{0:T(1024)(128)(4,1)S(1)}, s32[]{:S(2)}) async-start(s8[8388608]{0:T(1024)(128)(4,1)} %bitcast.303), calls=%async_computation | async-start | bytes 8388608
  412.2 20.7 %collective-permute-start.9 = (bf16[2,2,2,64,768]{4,3,0,1,2:T(8,128)(2,1)}, bf16[2,2,2,64,768]{4,3,0,1,2:T(8,128)(2,1)}, u32[]{:S(2)}, u32[]{:S(2)}) collective-permute-start(bf16[2,2,2,64,768]{4,3,0,1,2:T(8,128)(2,1)} %fusion.45), channel_id=1, source_target_pairs={{0,2},{2,0},{4,6},{6,4},{8,10},{10,8},{12,14},{14,12},{16,18},{18,... | collective-permute-start | bytes 2359304 | tf_op jit(solution)/shard_map/ppermute | solution.py:487
  415.2 6.2 %slice-start.1 = ((s8[8388608]{0:T(1024)(128)(4,1)}), s8[4194304]{0:T(1024)(128)(4,1)S(1)}, s32[]{:S(2)}) async-start(s8[8388608]{0:T(1024)(128)(4,1)} %bitcast.303), calls=%async_computation.1 | async-start | bytes 8388608
  415.2 80.3 %collective-permute-start.21 = (bf16[2,2,2,64,1280]{4,3,2,1,0:T(8,128)(2,1)}, bf16[2,2,2,64,1280]{4,3,2,1,0:T(8,128)(2,1)}, u32[]{:S(2)}, u32[]{:S(2)}) collective-permute-start(bf16[2,2,2,64,1280]{4,3,2,1,0:T(8,128)(2,1)} %fusion.10), channel_id=1, source_target_pairs={{0,2},{2,0},{4,6},{6,4},{8,10},{10,8},{12,14},{14,12},{16,18},{18,... | collective-permute-start | bytes 3932168 | tf_op jit(solution)/shard_map/ppermute | solution.py:487
  419.9 77.4 %collective-permute-start.17 = (bf16[2,2,2,64,1280]{4,3,0,1,2:T(8,128)(2,1)}, bf16[2,2,2,64,1280]{4,3,0,1,2:T(8,128)(2,1)}, u32[]{:S(2)}, u32[]{:S(2)}) collective-permute-start(bf16[2,2,2,64,1280]{4,3,0,1,2:T(8,128)(2,1)} %fusion.11), channel_id=1, source_target_pairs={{0,4},{2,6},{4,0},{6,2},{8,12},{10,14},{12,8},{14,10},{16,20},{18,... | collective-permute-start | bytes 3932168 | tf_op jit(solution)/shard_map/ppermute | solution.py:487
  424.2 9.7 %copy-start.10 = (f32[2,2,2,2,64,768]{5,4,3,2,1,0:T(8,128)S(1)}, f32[2,2,2,2,64,768]{5,4,3,2,1,0:T(8,128)}, u32[]{:S(2)}) copy-start(f32[2,2,2,2,64,768]{5,4,3,2,1,0:T(8,128)} %get-tuple-element.75) | copy-start | bytes 9437188
  424.3 92.4 %collective-permute-start.26 = (bf16[2,2,64,2048]{3,2,1,0:T(8,128)(2,1)S(1)}, bf16[2,2,64,2048]{3,2,1,0:T(8,128)(2,1)S(1)}, u32[]{:S(2)}, u32[]{:S(2)}) collective-permute-start(bf16[2,2,64,2048]{3,2,1,0:T(8,128)(2,1)S(1)} %fusion.21), channel_id=1, source_target_pairs={{0,2},{2,0},{4,6},{6,4},{8,10},{10,8},{12,14},{14,12},{16,18},{18,... | collective-permute-start | bytes 3145736 | tf_op jit(solution)/shard_map/ppermute | solution.py:487
  432.9 58.2 %collective-permute-start.14 = (bf16[2,2,64,768]{3,2,1,0:T(8,128)(2,1)S(1)}, bf16[2,2,64,768]{3,2,1,0:T(8,128)(2,1)S(1)}, u32[]{:S(2)}, u32[]{:S(2)}) collective-permute-start(bf16[2,2,64,768]{3,2,1,0:T(8,128)(2,1)S(1)} %fusion.61), channel_id=1, source_target_pairs={{0,2},{2,0},{4,6},{6,4},{8,10},{10,8},{12,14},{14,12},{16,18},{18,... | collective-permute-start | bytes 1179656 | tf_op jit(solution)/shard_map/ppermute | solution.py:487
  435.4 57.3 %collective-permute-start.10 = (bf16[2,2,64,768]{3,2,0,1:T(8,128)(2,1)S(1)}, bf16[2,2,64,768]{3,2,0,1:T(8,128)(2,1)S(1)}, u32[]{:S(2)}, u32[]{:S(2)}) collective-permute-start(bf16[2,2,64,768]{3,2,0,1:T(8,128)(2,1)S(1)} %fusion.60), channel_id=1, source_target_pairs={{0,4},{2,6},{4,0},{6,2},{8,12},{10,14},{12,8},{14,10},{16,20},{18,... | collective-permute-start | bytes 1179656 | tf_op jit(solution)/shard_map/ppermute | solution.py:487
  491.1 27.7 %collective-permute-start.30 = (bf16[2,2,64,2048]{3,2,1,0:T(8,128)(2,1)S(1)}, bf16[2,2,64,2048]{3,2,1,0:T(8,128)(2,1)S(1)}, u32[]{:S(2)}, u32[]{:S(2)}) collective-permute-start(bf16[2,2,64,2048]{3,2,1,0:T(8,128)(2,1)S(1)} %fusion.22), channel_id=1, source_target_pairs={{0,4},{2,6},{4,0},{6,2},{8,12},{10,14},{12,8},{14,10},{16,20},{18,... | collective-permute-start | bytes 3145736 | tf_op jit(solution)/shard_map/ppermute | solution.py:487
  492.7 8.5 %collective-permute-start.15 = (bf16[2,64,768]{2,1,0:T(8,128)(2,1)S(1)}, bf16[2,64,768]{2,1,0:T(8,128)(2,1)S(1)}, u32[]{:S(2)}, u32[]{:S(2)}) collective-permute-start(bf16[2,64,768]{2,1,0:T(8,128)(2,1)S(1)} %fusion.93), channel_id=1, source_target_pairs={{0,8},{2,10},{4,12},{6,14},{8,0},{10,2},{12,4},{14,6},{16,24},{18,... | collective-permute-start | bytes 589832 | tf_op jit(solution)/shard_map/ppermute | solution.py:487
  495.5 8.3 %collective-permute-start.11 = (bf16[2,64,768]{2,1,0:T(8,128)(2,1)S(1)}, bf16[2,64,768]{2,1,0:T(8,128)(2,1)S(1)}, u32[]{:S(2)}, u32[]{:S(2)}) collective-permute-start(bf16[2,64,768]{2,1,0:T(8,128)(2,1)S(1)} %fusion.92), channel_id=1, source_target_pairs={{0,8},{2,10},{4,12},{6,14},{8,0},{10,2},{12,4},{14,6},{16,24},{18,... | collective-permute-start | bytes 589832 | tf_op jit(solution)/shard_map/ppermute | solution.py:487
  497.3 32.3 %collective-permute-start.22 = (bf16[2,2,64,1280]{3,2,1,0:T(8,128)(2,1)S(1)}, bf16[2,2,64,1280]{3,2,1,0:T(8,128)(2,1)S(1)}, u32[]{:S(2)}, u32[]{:S(2)}) collective-permute-start(bf16[2,2,64,1280]{3,2,1,0:T(8,128)(2,1)S(1)} %fusion.47), channel_id=1, source_target_pairs={{0,4},{2,6},{4,0},{6,2},{8,12},{10,14},{12,8},{14,10},{16,20},{18,... | collective-permute-start | bytes 1966088 | tf_op jit(solution)/shard_map/ppermute | solution.py:487
  501.2 31.3 %collective-permute-start.18 = (bf16[2,2,64,1280]{3,2,0,1:T(8,128)(2,1)S(1)}, bf16[2,2,64,1280]{3,2,0,1:T(8,128)(2,1)S(1)}, u32[]{:S(2)}, u32[]{:S(2)}) collective-permute-start(bf16[2,2,64,1280]{3,2,0,1:T(8,128)(2,1)S(1)} %fusion.46), channel_id=1, source_target_pairs={{0,2},{2,0},{4,6},{6,4},{8,10},{10,8},{12,14},{14,12},{16,18},{18,... | collective-permute-start | bytes 1966088 | tf_op jit(solution)/shard_map/ppermute | solution.py:487
  503.8 5.5 collective-permute-start.16
  509.3 5.5 collective-permute-start.12
  517.0 15.8 %collective-permute-start.27 = (bf16[2,64,2048]{2,1,0:T(8,128)(2,1)S(1)}, bf16[2,64,2048]{2,1,0:T(8,128)(2,1)S(1)}, u32[]{:S(2)}, u32[]{:S(2)}) collective-permute-start(bf16[2,64,2048]{2,1,0:T(8,128)(2,1)S(1)} %fusion.57), channel_id=1, source_target_pairs={{0,8},{2,10},{4,12},{6,14},{8,0},{10,2},{12,4},{14,6},{16,24},{18,... | collective-permute-start | bytes 1572872 | tf_op jit(solution)/shard_map/ppermute | solution.py:487
  519.3 32.3 %collective-permute-start.31 = (bf16[2,64,2048]{2,1,0:T(8,128)(2,1)S(1)}, bf16[2,64,2048]{2,1,0:T(8,128)(2,1)S(1)}, u32[]{:S(2)}, u32[]{:S(2)}) collective-permute-start(bf16[2,64,2048]{2,1,0:T(8,128)(2,1)S(1)} %fusion.58), channel_id=1, source_target_pairs={{0,8},{2,10},{4,12},{6,14},{8,0},{10,2},{12,4},{14,6},{16,24},{18,... | collective-permute-start | bytes 1572872 | tf_op jit(solution)/shard_map/ppermute | solution.py:487
  529.8 30.2 %collective-permute-start.23 = (bf16[2,64,1280]{2,1,0:T(8,128)(2,1)S(1)}, bf16[2,64,1280]{2,1,0:T(8,128)(2,1)S(1)}, u32[]{:S(2)}, u32[]{:S(2)}) collective-permute-start(bf16[2,64,1280]{2,1,0:T(8,128)(2,1)S(1)} %fusion.63), channel_id=1, source_target_pairs={{0,8},{2,10},{4,12},{6,14},{8,0},{10,2},{12,4},{14,6},{16,24},{18,... | collective-permute-start | bytes 983048 | tf_op jit(solution)/shard_map/ppermute | solution.py:487
  532.7 31.5 %collective-permute-start.19 = (bf16[2,64,1280]{2,1,0:T(8,128)(2,1)S(1)}, bf16[2,64,1280]{2,1,0:T(8,128)(2,1)S(1)}, u32[]{:S(2)}, u32[]{:S(2)}) collective-permute-start(bf16[2,64,1280]{2,1,0:T(8,128)(2,1)S(1)} %fusion.62), channel_id=1, source_target_pairs={{0,8},{2,10},{4,12},{6,14},{8,0},{10,2},{12,4},{14,6},{16,24},{18,... | collective-permute-start | bytes 983048 | tf_op jit(solution)/shard_map/ppermute | solution.py:487
  533.0 31.5 %collective-permute-start.28 = (bf16[64,2048]{1,0:T(8,128)(2,1)S(1)}, bf16[64,2048]{1,0:T(8,128)(2,1)S(1)}, u32[]{:S(2)}, u32[]{:S(2)}) collective-permute-start(bf16[64,2048]{1,0:T(8,128)(2,1)S(1)} %fusion.64), channel_id=1, source_target_pairs={{0,16},{2,18},{4,20},{6,22},{8,24},{10,26},{12,28},{14,30},{16,0},... | collective-permute-start | bytes 786440 | tf_op jit(solution)/shard_map/ppermute | solution.py:487
  551.8 31.6 %collective-permute-start.32 = (bf16[64,2048]{1,0:T(8,128)(2,1)S(1)}, bf16[64,2048]{1,0:T(8,128)(2,1)S(1)}, u32[]{:S(2)}, u32[]{:S(2)}) collective-permute-start(bf16[64,2048]{1,0:T(8,128)(2,1)S(1)} %fusion.65), channel_id=1, source_target_pairs={{0,16},{2,18},{4,20},{6,22},{8,24},{10,26},{12,28},{14,30},{16,0},... | collective-permute-start | bytes 786440 | tf_op jit(solution)/shard_map/ppermute | solution.py:487
  560.1 19.5 %collective-permute-start.24 = (bf16[64,1280]{1,0:T(8,128)(2,1)S(1)}, bf16[64,1280]{1,0:T(8,128)(2,1)S(1)}, u32[]{:S(2)}, u32[]{:S(2)}) collective-permute-start(bf16[64,1280]{1,0:T(8,128)(2,1)S(1)} %fusion.95), channel_id=1, source_target_pairs={{0,16},{2,18},{4,20},{6,22},{8,24},{10,26},{12,28},{14,30},{16,0},... | collective-permute-start | bytes 491528 | tf_op jit(solution)/shard_map/ppermute | solution.py:487
  564.3 17.1 %collective-permute-start.20 = (bf16[64,1280]{1,0:T(8,128)(2,1)S(1)}, bf16[64,1280]{1,0:T(8,128)(2,1)S(1)}, u32[]{:S(2)}, u32[]{:S(2)}) collective-permute-start(bf16[64,1280]{1,0:T(8,128)(2,1)S(1)} %fusion.94), channel_id=1, source_target_pairs={{0,16},{2,18},{4,20},{6,22},{8,24},{10,26},{12,28},{14,30},{16,0},... | collective-permute-start | bytes 491528 | tf_op jit(solution)/shard_map/ppermute | solution.py:487
  579.6 5.4 copy-start.1
  583.2 1.2 collective-permute-start.33
  (16 other events, 23.9 us)

commit v2 on v1

--- a/solution.py
+++ b/solution.py
@@ -229,83 +229,6 @@
     )(query, qkv, qkv, code, qseg, qpos)
 
 
-def self_backward_body(block, parts, q_ref, k_ref, v_ref, code_ref, qseg_ref, qpos_ref, *rest):
-    grad_ref, out_ref, log_ref, dq_ref, dkv_ref, key_ref, value_ref, dk_ref, dv_ref = rest
-    step = pl.program_id(0)
-
-    @pl.when(step == 0)
-    def _():
-        key_ref[...] = k_ref[0].T
-        value_ref[...] = v_ref[0].T
-        dk_ref[...] = jnp.zeros_like(dk_ref)
-        dv_ref[...] = jnp.zeros_like(dv_ref)
-
-    query, grad = q_ref[0], grad_ref[0]
-    width = query.shape[1]
-    segments, positions, logs = qseg_ref[...], qpos_ref[...], log_ref[...]
-    row_dot = jnp.sum(grad.astype(F32) * out_ref[...], axis=0, keepdims=True)
-
-    def fold(index, dq, causal):
-        start = pl.multiple_of(index * block, block)
-        here = pl.ds(start, block)
-        scores = jnp.dot(key_ref[here, :], query, preferred_element_type=F32)
-        allowed = code_ref[here, :] == segments
-        if causal:
-            places = start + lax.broadcasted_iota(jnp.int32, (block, width), 0)
-            allowed = allowed & (places <= positions)
-        weights = jnp.where(allowed, jnp.exp2(scores * EXP2_SCALE - logs), 0.0)
-        weight_grad = jnp.dot(value_ref[here, :], grad, preferred_element_type=F32)
-        score_grad = (weights * (weight_grad - row_dot)).astype(BF16)
-        dv_ref[:, here] += dot(grad, weights.astype(BF16), 1, 1)
-        dk_ref[:, here] += dot(query, score_grad, 1, 1)
-        return dq + jnp.dot(k_ref[0, :, here], score_grad, preferred_element_type=F32)
-
-    dq = jnp.zeros((HEAD_DIM, width), F32)
-    dq = lax.fori_loop(0, step * parts, lambda i, s: fold(i, s, False), dq)
-    for part in range(parts):
-        dq = fold(step * parts + part, dq, True)
-    dq_ref[0] = (dq * SCALE).astype(BF16)
-
-    @pl.when(step == pl.num_programs(0) - 1)
-    def _():
-        dkv_ref[0] = (dk_ref[...] * SCALE).astype(BF16)
-        dkv_ref[1] = dv_ref[...].astype(BF16)
-
-
-def self_backward(query, qkv, code, qseg, qpos, grad, out, log, parts):
-    total, width = qkv.shape[2], query.shape[2]
-    block = min(512, width)
-    row = pl.BlockSpec((1, block), lambda i: (0, i))
-    column = pl.BlockSpec((1, HEAD_DIM, block), lambda i: (0, 0, i))
-    return pl.pallas_call(
-        functools.partial(self_backward_body, block, parts),
-        grid=(width // block,),
-        in_specs=[
-            column,
-            pl.BlockSpec((1, HEAD_DIM, total), lambda i: (1, 0, 0)),
-            pl.BlockSpec((1, HEAD_DIM, total), lambda i: (2, 0, 0)),
-            pl.BlockSpec((total, 1), lambda i: (0, 0)),
-            row,
-            row,
-            column,
-            pl.BlockSpec((HEAD_DIM, block), lambda i: (0, i)),
-            row,
-        ],
-        out_specs=[column, pl.BlockSpec((2, HEAD_DIM, total), lambda i: (0, 0, 0))],
-        out_shape=[
-            jax.ShapeDtypeStruct((1, HEAD_DIM, width), BF16),
-            jax.ShapeDtypeStruct((2, HEAD_DIM, total), BF16),
-        ],
-        scratch_shapes=[
-            pltpu.VMEM((total, HEAD_DIM), BF16),
-            pltpu.VMEM((total, HEAD_DIM), BF16),
-            pltpu.VMEM((HEAD_DIM, total), F32),
-            pltpu.VMEM((HEAD_DIM, total), F32),
-        ],
-        compiler_params=pltpu.CompilerParams(vmem_limit_bytes=VMEM_LIMIT),
-    )(query, qkv, qkv, code, qseg, qpos, grad, out, log)
-
-
 def page_rows(span, piece, real):
     places = lax.broadcasted_iota(jnp.int32, (span, 1), 0)
     return lax.rem(places, piece) < real
@@ -372,75 +295,570 @@
     )(low, high, query, kv, qseg)
 
 
-def cross_backward_body(piece, real, low_ref, high_ref, q_ref, kv_ref, qseg_ref, *rest):
-    grad_ref, out_ref, log_ref, dq_ref, dkv_ref, key_ref, value_ref, acc_ref = rest
-    step = pl.program_id(0)
-
-    @pl.when(step == 0)
-    def _():
-        for slot in range(NSEG):
-            key_ref[slot] = kv_ref[slot, 0].T
-            value_ref[slot] = kv_ref[slot, 1].T
-        acc_ref[...] = jnp.zeros_like(acc_ref)
-
-    query, grad, segments, logs = q_ref[0], grad_ref[0], qseg_ref[...], log_ref[...]
-    width, span = query.shape[1], kv_ref.shape[3]
-    row_dot = jnp.sum(grad.astype(F32) * out_ref[...], axis=0, keepdims=True)
-    present = page_rows(span, piece, real)
-
-    def fold(slot, dq):
-        scores = jnp.dot(key_ref[slot], query, preferred_element_type=F32)
-        allowed = present & (segments == slot)
-        weights = jnp.where(allowed, jnp.exp2(scores * EXP2_SCALE - logs), 0.0)
-        weight_grad = jnp.dot(value_ref[slot], grad, preferred_element_type=F32)
+class Copies:
+    def __init__(self, send_sem, recv_sem):
+        self.send_sem, self.recv_sem, self.used = send_sem, recv_sem, 0
+
+    def remote(self, source, target, device):
+        index, self.used = self.used, self.used + 1
+        copy = pltpu.make_async_remote_copy(
+            src_ref=source,
+            dst_ref=target,
+            send_sem=self.send_sem.at[index],
+            recv_sem=self.recv_sem.at[index],
+            device_id=device,
+            device_id_type=MESH,
+        )
+        copy.start()
+        return copy
+
+    def local(self, source, target):
+        index, self.used = self.used, self.used + 1
+        copy = pltpu.make_async_copy(source, target, self.send_sem.at[index])
+        copy.start()
+        return copy
+
+
+def wait_all(copies):
+    for copy in copies:
+        copy.wait()
+
+
+def reversed_bits(value, bits):
+    return sum(((value >> b) & 1) << (bits - 1 - b) for b in range(bits))
+
+
+class Halving:
+    def __init__(self, copies, me, count, sums, arrivals):
+        self.copies, self.me = copies, me
+        self.bits = count.bit_length() - 1
+        self.sums, self.arrivals = sums, arrivals
+        self.quarter = sums.shape[1] // 2
+        self.jobs, self.pending = [], []
+
+    def neighbour(self, kind, step):
+        bit = 1 - step if kind == 1 and step < 2 else step
+        return {"blk": self.me ^ (1 << bit)}
+
+    def add_job(self, column, width, make):
+        here, started = pl.ds(column, width), []
+        for kind in range(2):
+            for half, quarter in enumerate((2, 3) if kind == 0 else (1, 3)):
+                rows = pl.ds(half * self.quarter, self.quarter)
+                self.sums[kind, rows, here] = make(kind, quarter).astype(BF16)
+            started.append(
+                self.copies.remote(
+                    self.sums.at[kind, :, here],
+                    self.arrivals[0].at[kind, :, here],
+                    self.neighbour(kind, 0),
+                )
+            )
+        self.jobs.append((here, make, started))
+
+    def keep_jobs(self):
+        for here, make, started in self.jobs:
+            wait_all(started)
+            for kind in range(2):
+                for half, quarter in enumerate((0, 1) if kind == 0 else (0, 2)):
+                    rows = pl.ds(half * self.quarter, self.quarter)
+                    arrived = self.arrivals[0][kind, rows, here].astype(F32)
+                    self.sums[kind, rows, here] = (make(kind, quarter) + arrived).astype(BF16)
+
+    def send(self, step):
+        rows = self.sums.shape[1] >> step
+        self.pending = [
+            self.copies.remote(
+                self.sums.at[kind, pl.ds(rows, rows), :],
+                self.arrivals[step].at[kind],
+                self.neighbour(kind, step),
+            )
+            for kind in range(2)
+        ]
+
+    def receive(self, step, result=None):
+        rows = self.sums.shape[1] >> step
+        wait_all(self.pending)
+        size = min(rows, 32)
+
+        def add(index, _):
+            here = pl.ds(pl.multiple_of(index * size, size), size)
+            for kind in range(2):
+                mine = self.sums[kind, here, :].astype(F32)
+                total = mine + self.arrivals[step][kind, here, :].astype(F32)
+                if result is None:
+                    self.sums[kind, here, :] = total.astype(BF16)
+                else:
+                    result[kind, here, :] = total
+            return 0
+
+        lax.fori_loop(0, rows // size, add, 0)
+
+
+def arrivals_shapes(count, width, columns):
+    bits = count.bit_length() - 1
+    return [pltpu.VMEM((2, width >> (step + 1), columns), BF16) for step in range(bits)]
+
+
+def norm_back_rows(target, grad, unit, inv_std, gain, residual, low=None):
+    step = 32
+
+    def body(index, _):
+        rows = pl.ds(pl.multiple_of(index * step, step), step)
+        z = unit[rows, :]
+        w = grad(rows) * gain[...]
+        inner = w - jnp.mean(w, axis=1, keepdims=True) - z * jnp.mean(w * z, axis=1, keepdims=True)
+        value = residual[rows, :] + inner * inv_std[rows, :]
+        target[rows, :] = value
+        if low is not None:
+            low[rows, :] = value.astype(BF16)
+        return 0
+
+    lax.fori_loop(0, target.shape[0] // step, body, 0)
+
+
+def backward_body(lay, names, late, scratch_names, *refs):
+    r = dict(zip(names, refs, strict=False))
+    outs = refs[len(names) : len(names) + 6]
+    grad_input, memory_own, memory_other, feed_out, middle_out, first_out = outs
+    s = dict(zip(scratch_names, refs[len(names) + 6 :], strict=True))
+    count, parts, half, rows = lay.count, lay.parts, lay.half, lay.rows
+    me, core = lax.axis_index("blk"), lax.axis_index("tp")
+    bits = count.bit_length() - 1
+    width, wide = r["dc"].shape[1], r["w_cross_out"].shape[0]
+    flat_rows = r["dc"].shape[0]
+    total, mine_total = r["qkv"].shape[2], r["qkv"].shape[2] // parts
+    block = min(512 if parts == 1 else 256, mine_total)
+
+    barrier = pltpu.get_barrier_semaphore()
+    for offset in range(1, count):
+        pl.semaphore_signal(barrier, inc=1, device_id={"blk": me ^ offset}, device_id_type=MESH)
+    pl.semaphore_signal(barrier, inc=1, device_id={"tp": 1 - core}, device_id_type=MESH)
+    copies = Copies(s["send_sem"], s["recv_sem"])
+    loading = {}
+
+    def load(name):
+        loading[name] = copies.local(r[name], s["in_" + late[name]])
+
+    for name, home in late.items():
+        if name == home:
+            load(name)
+
+    def ready(*wanted):
+        for name in wanted:
+            loading[name].wait()
+            r[name] = s["in_" + late[name]]
+
+    def to_other_core(sent, arrived):
+        return copies.remote(sent, arrived, {"tp": 1 - core})
+
+    head, pack, part = lay.head(me), me // half, lax.rem(me, parts)
+
+    def spread(source, target):
+        started = []
+        for offset in range(0, count, parts):
+            peer = me ^ offset
+            piece = source.at[
+                pl.ds(lay.head(peer) * HEAD_DIM, HEAD_DIM), pl.ds((peer // half) * rows, rows)
+            ]
+            place = target.at[:, pl.ds((me // parts) * rows, rows)]
+            if offset == 0:
+                started.append(copies.local(piece, place))
+            else:
+                started.append(copies.remote(piece, place, {"blk": peer}))
+        return started
+
+    def collect(source, target):
+        started = []
+        place = target.at[pl.ds(head * HEAD_DIM, HEAD_DIM), pl.ds(pack * rows, rows)]
+        for offset in range(0, count, parts):
+            peer = me ^ offset
+            piece = source.at[:, pl.ds((peer // parts) * rows, rows)]
+            if offset == 0:
+                started.append(copies.local(piece, place))
+            else:
+                started.append(copies.remote(piece, place, {"blk": peer}))
+        return started
+
+    def relative(target, value):
+        share, most = width // count, s["turn"].shape[1]
+        for start in range(0, value.shape[0], most):
+            size = min(most, value.shape[0] - start)
+            s["turn"][:, :size] = value[start : start + size, :].T
+            for place in range(count):
+                chunk = me ^ reversed_bits(place, bits)
+                target[pl.ds(place * share, share), start : start + size] = s["turn"][
+                    pl.ds(pl.multiple_of(chunk * share, share), share), :size
+                ]
+
+    quarter = width // 4
+
+    def quarter_of(ref, index):
+        return ref[pl.ds(index * quarter, quarter), :]
+
+    ready("w_cross_out")
+    s["out_small"][0] = dot(r["w_cross_out"][...], r["dc"][...], 1, 1).astype(BF16)
+    pl.semaphore_wait(barrier, count)
+    doc_copies = spread(s["out_small"].at[0], s["doc_unit"])
+    load("w_out")
+
+    feed = Halving(
+        copies, me, count, s["feed_sums"], [s[f"feed_{i}"] for i in range(bits)]
+    )
+    ready("dm", "gelu", "h3", "du")
+    relative(s["rel_dm"], r["dm"])
+    relative(s["rel_h3"], r["h3"])
+    load("h2")
+    load("h1")
+    step = 512
+    for column in range(0, r["gelu"].shape[1], step):
+
+        def make(kind, index, column=column):
+            left, right = (("rel_dm", "gelu"), ("rel_h3", "du"))[kind]
+            return dot(quarter_of(s[left], index), r[right][:, column : column + step], 1, 0)
+
+        feed.add_job(column, step, make)
+
+    ready("kv_slots", "cross_unit", "cross_att")
+    slots, span = r["kv_slots"].shape[0], r["kv_slots"].shape[3]
+    s["cross_key"][...] = r["kv_slots"][0, 0].T
+    s["cross_value"][...] = r["kv_slots"][0, 1].T
+    s["cross_acc"][...] = jnp.zeros_like(s["cross_acc"])
+    present = page_rows(span, lay.mem_pad, lay.mem_rows)
+    wait_all(doc_copies)
+
+    def cross_block(here, slot, key_rows, value_rows):
+        query, grad = r["cross_unit"][0, :, here], s["doc_unit"][:, here]
+        row_dot = jnp.sum(grad.astype(F32) * r["cross_att"][:, here], axis=0, keepdims=True)
+        scores = jnp.dot(key_rows, query, preferred_element_type=F32)
+        allowed = present & (r["qslot"][:, here] == slot)
+        weights = jnp.where(
+            allowed, jnp.exp2(scores * EXP2_SCALE - r["cross_log"][:, here]), 0.0
+        )
+        weight_grad = jnp.dot(value_rows, grad, preferred_element_type=F32)
         score_grad = (weights * (weight_grad - row_dot)).astype(BF16)
-        acc_ref[slot, 1] += dot(grad, weights.astype(BF16), 1, 1)
-        acc_ref[slot, 0] += dot(query, score_grad, 1, 1)
-        return dq + jnp.dot(kv_ref[slot, 0], score_grad, preferred_element_type=F32)
-
-    dq = jnp.zeros((HEAD_DIM, width), F32)
-    dq = lax.fori_loop(low_ref[step], high_ref[step] + 1, fold, dq)
-    dq_ref[0] = (dq * SCALE).astype(BF16)
-
-    @pl.when(step == pl.num_programs(0) - 1)
-    def _():
-        for slot in range(NSEG):
-            dkv_ref[slot, 0] = (acc_ref[slot, 0] * SCALE).astype(BF16)
-            dkv_ref[slot, 1] = acc_ref[slot, 1].astype(BF16)
-
-
-def cross_backward(query, kv, qseg, low, high, grad, out, log, piece, real):
-    width, span = query.shape[2], kv.shape[3]
-    block = min(512, width)
-    row = pl.BlockSpec((1, block), lambda i, *_: (0, i))
-    column = pl.BlockSpec((1, HEAD_DIM, block), lambda i, *_: (0, 0, i))
-    pages = pl.BlockSpec((NSEG, 2, HEAD_DIM, span), lambda i, *_: (0, 0, 0, 0))
+        dq = jnp.dot(r["kv_slots"][slot, 0], score_grad, preferred_element_type=F32)
+        return dq, dot(query, score_grad, 1, 1), dot(grad, weights.astype(BF16), 1, 1)
+
+    narrow = min(256, mine_total)
+
+    def main_slot(index, _):
+        here = pl.ds(pl.multiple_of(index * narrow, narrow), narrow)
+        dq, dk, dv = cross_block(here, 0, s["cross_key"][...], s["cross_value"][...])
+        s["dq_acc"][:, here] = dq
+        s["cross_acc"][0] += dk
+        s["cross_acc"][1] += dv
+        return 0
+
+    lax.fori_loop(0, mine_total // narrow, main_slot, 0)
+    s["dkv_low"][0, 0, 0] = (s["cross_acc"][0] * SCALE).astype(BF16)
+    s["dkv_low"][0, 0, 1] = s["cross_acc"][1].astype(BF16)
+    for slot in range(1, slots):
+        key_rows, value_rows = r["kv_slots"][slot, 0].T, r["kv_slots"][slot, 1].T
+        ends = []
+        for start in (0, mine_total - LANES):
+            here = pl.ds(start, LANES)
+            ends.append(cross_block(here, slot, key_rows, value_rows))
+            s["dq_acc"][:, here] += ends[-1][0]
+        s["dkv_low"][0, slot, 0] = ((ends[0][1] + ends[1][1]) * SCALE).astype(BF16)
+        s["dkv_low"][0, slot, 1] = (ends[0][2] + ends[1][2]).astype(BF16)
+    load("att")
+    s["dq_low"][0] = (s["dq_acc"][...] * SCALE).astype(BF16)
+    dqc_copies = collect(s["dq_low"].at[0], s["in_small"].at[0])
+    twin = copies.remote(
+        s["dkv_low"].at[0], s["dkv_low"].at[1], {"blk": lax.rem(me + half, count)}
+    )
+
+    middle = Halving(
+        copies, me, count, s["middle_sums"], [s[f"middle_{i}"] for i in range(bits)]
+    )
+    piece = wide // 2
+
+    def weight_job(batch, place, left, right):
+        def make(kind, index):
+            return dot(quarter_of(left, index), right[kind * piece : (kind + 1) * piece, :], 1, 1)
+
+        batch.add_job(place * piece, piece, make)
+
+    ready("cross_mixed")
+    relative(s["rel_dc"], r["dc"])
+    weight_job(middle, 0, s["rel_dc"], r["cross_mixed"])
+
+    ready("w_cross_query", "unit_two", "grad_two")
+    wait_all(dqc_copies)
+    for start in range(0, flat_rows, LANES):
+        here = slice(start, start + LANES)
+        s["tp_send"][here, :] = dot(s["in_small"][0, :, here].T, r["w_cross_query"][...], 1, 1).astype(
+            BF16
+        )
+    tp_copy = to_other_core(s["tp_send"], s["tp_recv"].at[0])
+    ready("h2")
+    relative(s["rel_h2"], r["h2"])
+    weight_job(middle, 1, s["rel_h2"], s["in_small"].at[0])
+    tp_copy.wait()
+
+    def both_cores(index):
+        def grad(here):
+            return s["tp_send"][here, :].astype(F32) + s["tp_recv"][index, here, :].astype(F32)
+
+        return grad
+
+    norm_back_rows(
+        s["grad_one"], both_cores(0), r["unit_two"], r["inv_two"], r["gain_two"], r["grad_two"], s["da"]
+    )
+    ready("w_out")
+    s["out_small"][1] = dot(r["w_out"][...], s["da"][...], 1, 1).astype(BF16)
+    for name in ("w_q", "unit_one"):
+        load(name)
+    do_copies = spread(s["out_small"].at[1], s["do_unit"])
+    ready("mixed")
+    relative(s["rel_da"], s["da"])
+    weight_job(middle, 2, s["rel_da"], r["mixed"])
+
+    twin.wait()
+    pages_here = lay.pages_half
+    for page in range(pages_here):
+        for piece_index in range(lay.pieces):
+            here = slice(piece_index * lay.mem_pad, (piece_index + 1) * lay.mem_pad)
+            value = None
+            for side in range(2):
+                for slot in range(slots):
+                    term = r["hot"][side, slot, page] * s["dkv_low"][side, slot, :, :, here].astype(F32)
+                    value = term if value is None else value + term
+            s["page_grad"][page * lay.pieces + piece_index] = value.astype(BF16)
+    memory_copies = []
+    for offset in range(half):
+        peer = me ^ offset
+        source = s["page_grad"].at[lax.rem(peer, half)]
+        place = s["mem_recv"].at[part, :, pl.ds(head * HEAD_DIM, HEAD_DIM), :]
+        if offset == 0:
+            memory_copies.append(copies.local(source, place))
+        else:
+            memory_copies.append(copies.remote(source, place, {"blk": peer}))
+
+    ready("qkv", "att")
+    if parts > 1:
+        ready("query")
+    query_ref = r["query"] if parts > 1 else r["qkv"]
+    feed.keep_jobs()
+    feed.send(1)
+    s["dq_acc"][...] = jnp.zeros_like(s["dq_acc"])
+    wait_all(do_copies)
+
+    def key_block(key_index, _):
+        here = pl.ds(pl.multiple_of(key_index * block, block), block)
+        keys, values = r["qkv"][1, :, here], r["qkv"][2, :, here]
+        key_rows, value_rows = keys.T, values.T
+        codes = jnp.broadcast_to(r["code"][:, here], (8, block)).T[:, :1]
+
+        def fold(index, grads, causal):
+            dk, dv = grads
+            columns = pl.ds(pl.multiple_of(index * block, block), block)
+            query, grad = query_ref[0, :, columns], s["do_unit"][:, columns]
+            row_dot = jnp.sum(grad.astype(F32) * r["att"][:, columns], axis=0, keepdims=True)
+            scores = jnp.dot(key_rows, query, preferred_element_type=F32)
+            allowed = codes == r["qseg"][:, columns]
+            if causal:
+                places = index * block + lax.broadcasted_iota(jnp.int32, (1, block), 1)
+                positions = ((places // rows) * parts + part) * rows + places % rows
+                key_places = key_index * block + lax.broadcasted_iota(
+                    jnp.int32, (block, block), 0
+                )
+                allowed = allowed & (key_places <= positions)
+            weights = jnp.where(allowed, jnp.exp2(scores * EXP2_SCALE - r["log"][:, columns]), 0.0)
+            weight_grad = jnp.dot(value_rows, grad, preferred_element_type=F32)
+            score_grad = (weights * (weight_grad - row_dot)).astype(BF16)
+            s["dq_acc"][:, columns] += jnp.dot(keys, score_grad, preferred_element_type=F32)
+            return (dk + dot(query, score_grad, 1, 1), dv + dot(grad, weights.astype(BF16), 1, 1))
+
+        zeros = jnp.zeros((HEAD_DIM, block), F32)
+        first_index = key_index // parts
+        grads = fold(first_index, (zeros, zeros), True)
+        dk, dv = lax.fori_loop(
+            first_index + 1, mine_total // block, lambda i, g: fold(i, g, False), grads
+        )
+        r["qkv"][1, :, here] = (dk * SCALE).astype(BF16)
+        r["qkv"][2, :, here] = dv.astype(BF16)
+        return 0
+
+    lax.fori_loop(0, total // block, key_block, 0)
+    s["dq_low"][1] = (s["dq_acc"][...] * SCALE).astype(BF16)
+    dq_copies = collect(s["dq_low"].at[1], s["in_small"].at[1])
+    dkv_copies = []
+    for offset in range(count):
+        peer = me ^ offset
+        source = r["qkv"].at[pl.ds(1, 2), :, pl.ds(peer * rows, rows)]
+        place = s["dkv_recv"].at[
+            part, :, pl.ds(head * HEAD_DIM, HEAD_DIM), pl.ds(pack * rows, rows)
+        ]
+        if offset == 0:
+            dkv_copies.append(copies.local(source, place))
+        else:
+            dkv_copies.append(copies.remote(source, place, {"blk": peer}))
+
+    ready("mem", "w_ck", "w_cv")
+    wait_all(memory_copies)
+    if parts > 1:
+        for kind in range(2):
+            value = s["mem_recv"][0, kind].astype(F32)
+            for index in range(1, parts):
+                value = value + s["mem_recv"][index, kind].astype(F32)
+            s["mem_recv"][0, kind] = value.astype(BF16)
+    for start in range(0, lay.mem_pad, LANES):
+        here = slice(start, start + LANES)
+        s["mem_send"][here, :] = (
+            dot(s["mem_recv"][0, 0, :, here].T, r["w_ck"][...], 1, 1)
+            + dot(s["mem_recv"][0, 1, :, here].T, r["w_cv"][...], 1, 1)
+        ).astype(BF16)
+    load("w_k")
+    load("w_v")
+    mem_copies = [
+        to_other_core(s["mem_send"], memory_other),
+        copies.local(s["mem_send"], memory_own),
+    ]
+    relative(s["rel_mem"], r["mem"])
+    weight_job(middle, 3, s["rel_mem"], s["mem_recv"].at[0, 0])
+    weight_job(middle, 4, s["rel_mem"], s["mem_recv"].at[0, 1])
+
+    feed.receive(1)
+    if bits > 2:
+        feed.send(2)
+    ready("w_q", "w_k", "w_v", "unit_one", "h1")
+    relative(s["rel_h3"], r["h1"])
+    wait_all(dq_copies)
+    wait_all(dkv_copies)
+    if parts > 1:
+        for kind in range(2):
+            value = s["dkv_recv"][0, kind].astype(F32)
+            for index in range(1, parts):
+                value = value + s["dkv_recv"][index, kind].astype(F32)
+            s["dkv_recv"][0, kind] = value.astype(BF16)
+    first = Halving(
+        copies,
+        me,
+        count,
+        s["feed_0"].at[:, :, pl.ds(0, 3 * wide // 2)],
+        [s[f"first_{i}"] for i in range(bits)],
+    )
+    pieces = (s["in_small"].at[1], s["dkv_recv"].at[0, 0], s["dkv_recv"].at[0, 1])
+    for place, value in enumerate(pieces):
+        weight_job(first, place, s["rel_h3"], value)
+    for start in range(0, flat_rows, LANES):
+        here = slice(start, start + LANES)
+        s["tp_send"][here, :] = sum(
+            dot(value[:, here].T, r[weight][...], 1, 1)
+            for value, weight in zip(pieces, ("w_q", "w_k", "w_v"), strict=True)
+        ).astype(BF16)
+    tp_copy = to_other_core(s["tp_send"], s["tp_recv"].at[1])
+    middle.keep_jobs()
+    middle.send(1)
+    tp_copy.wait()
+
+    def both_cores_two(here):
+        return s["tp_send"][here, :].astype(F32) + s["tp_recv"][1, here, :].astype(F32)
+
+    norm_back_rows(
+        grad_input, both_cores_two, r["unit_one"], r["inv_one"], r["gain_one"], s["grad_one"]
+    )
+
+    batches = [(feed, feed_out, 2), (middle, middle_out, 1), (first, first_out, 0)]
+    first.keep_jobs()
+    first.send(1)
+    middle.receive(1)
+    middle.send(2)
+    for step in range(2, bits):
+        last = step == bits - 1
+        feed.receive(step, feed_out if last else None)
+        if not last:
+            feed.send(step + 1)
+        first.receive(step - 1)
+        first.send(step)
+        middle.receive(step, middle_out if last else None)
+        if not last:
+            middle.send(step + 1)
+    first.receive(bits - 1, first_out)
+    wait_all(mem_copies)
+
+
+def backward(lay, values, hot, ff):
+    parts, count, half = lay.parts, lay.count, lay.half
+    width = values["dc"].shape[1]
+    flat_rows, wide = values["dc"].shape[0], lay.heads * HEAD_DIM
+    total = values["qkv"].shape[2]
+    mine_total = total // parts
+    span = lay.pieces * lay.mem_pad
+    bits = count.bit_length() - 1
+    if parts == 1:
+        values.pop("query")
+    late = [
+        "w_cross_out", "dm", "gelu", "h3", "du", "kv_slots", "cross_unit", "cross_att", "cross_mixed",
+        "w_cross_query", "unit_two", "grad_two", "mixed", "qkv", "mem",
+        "w_ck", "w_cv",
+    ]
+    if parts > 1:
+        late.append("query")
+    late = {name: name for name in late}
+    late.update(w_out="w_cross_out", w_q="w_cross_query", w_k="w_ck", w_v="w_cv")
+    late.update(unit_one="unit_two", h2="dm", h1="h3", att="cross_att")
+    early = [name for name in values if name not in late]
+    names = ["hot"] + early + list(late)
+    vmem, anywhere = pl.BlockSpec(memory_space=pltpu.VMEM), pl.BlockSpec(memory_space=pl.ANY)
+
+    def buffer(*shape, dtype=BF16):
+        return pltpu.VMEM(shape, dtype)
+
+    scratch = {
+        "send_sem": pltpu.SemaphoreType.DMA((7 * count + 96,)),
+        "recv_sem": pltpu.SemaphoreType.DMA((7 * count + 96,)),
+        "out_small": buffer(2, wide, flat_rows),
+        "in_small": buffer(2, wide, flat_rows),
+        "doc_unit": buffer(HEAD_DIM, mine_total),
+        "do_unit": buffer(HEAD_DIM, mine_total),
+        "dq_acc": buffer(HEAD_DIM, mine_total, dtype=F32),
+        "dq_low": buffer(2, HEAD_DIM, mine_total),
+        "turn": buffer(width, flat_rows),
+        "rel_dm": buffer(width, flat_rows),
+        "rel_h3": buffer(width, flat_rows),
+        "rel_dc": buffer(width, flat_rows),
+        "rel_h2": buffer(width, flat_rows),
+        "rel_da": buffer(width, flat_rows),
+        "rel_mem": buffer(width, lay.mem_pad),
+        "cross_key": buffer(span, HEAD_DIM),
+        "cross_value": buffer(span, HEAD_DIM),
+        "cross_acc": buffer(2, HEAD_DIM, span, dtype=F32),
+        "dkv_low": buffer(2, NSEG, 2, HEAD_DIM, span),
+        "page_grad": buffer(half, 2, HEAD_DIM, lay.mem_pad),
+        "mem_recv": buffer(parts, 2, wide, lay.mem_pad),
+        "mem_send": buffer(lay.mem_pad, width),
+        "tp_send": buffer(flat_rows, width),
+        "tp_recv": buffer(2, flat_rows, width),
+        "grad_one": buffer(flat_rows, width, dtype=F32),
+        "da": buffer(flat_rows, width),
+        "dkv_recv": buffer(parts, 2, wide, flat_rows),
+    }
+    columns = {"feed": ff, "middle": 5 * wide // 2, "first": 3 * wide // 2}
+    for name, number in columns.items():
+        if name != "first":
+            scratch[name + "_sums"] = buffer(2, width // 2, number)
+        for index, shape in enumerate(arrivals_shapes(count, width, number)):
+            scratch[f"{name}_{index}"] = shape
+    for name in dict.fromkeys(late.values()):
+        scratch["in_" + name] = pltpu.VMEM(values[name].shape, values[name].dtype)
+    share = width // count
     return pl.pallas_call(
-        functools.partial(cross_backward_body, piece, real),
-        grid_spec=pltpu.PrefetchScalarGridSpec(
-            num_scalar_prefetch=2,
-            grid=(width // block,),
-            in_specs=[
-                column,
-                pages,
-                row,
-                column,
-                pl.BlockSpec((HEAD_DIM, block), lambda i, *_: (0, i)),
-                row,
-            ],
-            out_specs=[column, pages],
-            scratch_shapes=[
-                pltpu.VMEM((NSEG, span, HEAD_DIM), BF16),
-                pltpu.VMEM((NSEG, span, HEAD_DIM), BF16),
-                pltpu.VMEM((NSEG, 2, HEAD_DIM, span), F32),
-            ],
+        functools.partial(backward_body, lay, names, late, list(scratch)),
+        out_shape=[
+            jax.ShapeDtypeStruct((flat_rows, width), F32),
+            jax.ShapeDtypeStruct((lay.mem_pad, width), BF16),
+            jax.ShapeDtypeStruct((lay.mem_pad, width), BF16),
+        ]
+        + [jax.ShapeDtypeStruct((2, share, columns[name]), F32) for name in columns],
+        in_specs=[pl.BlockSpec(memory_space=pltpu.SMEM)] + [vmem] * len(early) + [anywhere] * len(late),
+        out_specs=[vmem, anywhere, anywhere, vmem, vmem, vmem],
+        scratch_shapes=list(scratch.values()),
+        compiler_params=pltpu.CompilerParams(
+            collective_id=4, has_side_effects=True, vmem_limit_bytes=62 * 1024 * 1024
         ),
-        out_shape=[
-            jax.ShapeDtypeStruct((1, HEAD_DIM, width), BF16),
-            jax.ShapeDtypeStruct((NSEG, 2, HEAD_DIM, span), BF16),
-        ],
-        compiler_params=pltpu.CompilerParams(vmem_limit_bytes=VMEM_LIMIT),
-    )(low, high, query, kv, qseg, grad, out, log)
+    )(hot, *[values[name] for name in early + list(late)])
 
 
 def layer_norm(value, gain):
@@ -468,29 +886,6 @@
 def tp_total(partial_sum):
     low = partial_sum.astype(BF16)
     return low.astype(F32) + other_core(low).astype(F32)
-
-
-def reduce_scatter(grad, count, place):
-    bits = count.bit_length() - 1
-    rows, columns = grad.shape[0] // count, grad.shape[1]
-    grad = grad.reshape((2,) * bits + (rows, columns))
-
-    def run(piece, order):
-        left = list(range(bits - 1, -1, -1))
-        for bit in order:
-            axis = left.index(bit)
-            left.remove(bit)
-            mine = (place >> bit) & 1
-            keep = lax.dynamic_index_in_dim(piece, mine, axis, keepdims=False)
-            send = lax.dynamic_index_in_dim(piece, 1 - mine, axis, keepdims=False).astype(BF16)
-            pairs = [(i, i ^ (1 << bit)) for i in range(count)]
-            piece = keep.astype(F32) + lax.ppermute(send, "blk", pairs).astype(F32)
-        return piece
-
-    first = list(range(bits))
-    second = [1, 0] + first[2:]
-    half = columns // 2
-    return jnp.concatenate([run(grad[..., :half], first), run(grad[..., half:], second)], axis=-1)
 
 
 def local(
@@ -569,8 +964,12 @@
         .reshape(pages_here, 2, HEAD_DIM, lay.pieces * lay.mem_pad)
     )
     first_page = pack * pages_here
-    own_pages = lax.dynamic_index_in_dim(slot_pages, pack, 0, keepdims=False)
-    twin_pages = lax.dynamic_index_in_dim(slot_pages, 1 - pack, 0, keepdims=False)
+    longest = jnp.argmax(
+        jnp.sum((segments == jnp.arange(NSEG, dtype=jnp.int32)[:, None]).astype(jnp.int32), axis=1)
+    ).astype(jnp.int32)
+    own_pages = jnp.roll(lax.dynamic_index_in_dim(slot_pages, pack, 0, keepdims=False), -longest)
+    twin_pages = lax.ppermute(own_pages, "blk", [(i, (i + count // packs) % count) for i in range(count)])
+    query_slots = lax.rem(query_segments - longest + NSEG, NSEG)
 
     def pages_of(wanted):
         found = [
@@ -600,10 +999,10 @@
     (cross_unit,) = exchange(2, [lay.to_units(cross_tokens)])
     cross_unit = own_part(cross_unit)
     block = min(512, total // parts)
-    blocks = query_segments.reshape(-1, block)
-    low, high = blocks[:, 0], blocks[:, -1]
+    blocks = query_slots.reshape(-1, block)
+    low, high = jnp.min(blocks, axis=1), jnp.max(blocks, axis=1)
     cross_attention, cross_low, cross_log = cross_forward(
-        cross_unit, kv_slots, query_segments, low, high, lay.mem_pad, lay.mem_rows
+        cross_unit, kv_slots, query_slots, low, high, lay.mem_pad, lay.mem_rows
     )
     (cross_mixed,) = exchange(3, [lay.from_units(all_parts(cross_low))])
     cross_mixed = pick_part(cross_mixed)[0]
@@ -619,103 +1018,63 @@
     up_grad = gelu_back(dot(down_in, weight_down, 1, 1))[0].astype(BF16)
     grad_hidden = tp_total(dot(up_grad, weight_up, 1, 1))
     grad_two = down_in.astype(F32) + norm_back(grad_hidden, unit_three, inv_three, gain_three)
-    feed_share = reduce_scatter(
-        jnp.concatenate([dot(down_in, gelu_low, 0, 0), dot(hidden_three, up_grad, 0, 0)], axis=1),
-        count,
-        place,
-    )
-
-    cross_in = grad_two.astype(BF16)
-    cross_grad = dot(cross_out, cross_in, 1, 1).astype(BF16)[None]
-    (cross_grad,) = exchange(4, [lay.to_units(cross_grad)])
-    cross_dq, cross_dkv = cross_backward(
-        cross_unit,
-        kv_slots,
-        query_segments,
-        low,
-        high,
-        own_part(cross_grad),
-        cross_attention,
-        cross_log,
-        lay.mem_pad,
-        lay.mem_rows,
-    )
-    twin_dkv = lax.ppermute(cross_dkv, "blk", twin_pairs)
+
     page_ids = first_page + jnp.arange(pages_here, dtype=jnp.int32)
-    page_grad = sum(
-        jnp.where(
-            (pages[s] == page_ids)[:, None, None, None], grads[s].astype(F32)[None], 0.0
+    hot = (jnp.stack([own_pages, twin_pages])[:, :, None] == page_ids).astype(F32)
+    values = {
+        "dc": grad_two.astype(BF16),
+        "dm": down_in,
+        "gelu": gelu_low,
+        "h3": hidden_three,
+        "du": up_grad,
+        "grad_two": grad_two,
+        "unit_two": unit_two,
+        "inv_two": inv_two,
+        "gain_two": gain_two[None],
+        "unit_one": unit_one,
+        "inv_one": inv_one,
+        "gain_one": gain_one[None],
+        "h2": hidden_two,
+        "h1": hidden_one,
+        "mixed": mixed,
+        "cross_mixed": cross_mixed,
+        "mem": memory_padded,
+        "qkv": qkv,
+        "query": query,
+        "code": key_codes.reshape(1, total).astype(F32),
+        "qseg": query_segments.astype(F32),
+        "att": attention,
+        "log": attention_log,
+        "cross_unit": cross_unit,
+        "kv_slots": kv_slots,
+        "qslot": query_slots,
+        "cross_att": cross_attention,
+        "cross_log": cross_log,
+        "w_cross_out": cross_out,
+        "w_cross_query": cross_query,
+        "w_out": weight_out,
+        "w_ck": cross_key,
+        "w_cv": cross_value,
+        "w_q": weight_query,
+        "w_k": weight_key,
+        "w_v": weight_value,
+    }
+    grad_input, memory_own, memory_other, feed_share, middle_share, first_share = backward(
+        lay, values, hot, weight_up.shape[1]
+    )
+    grad_memory = (memory_own.astype(F32) + memory_other.astype(F32))[: lay.mem_rows]
+    grad_input = grad_input.reshape(packs, rows, width)
+
+    wide = weight_query.shape[1]
+    grad_down, grad_up = feed_share[0].T, feed_share[1]
+
+    def columns_of(value, index):
+        return jnp.concatenate(
+            [value[kind, :, index * wide // 2 : (index + 1) * wide // 2] for kind in range(2)], axis=1
         )
-        for pages, grads in ((own_pages, cross_dkv), (twin_pages, twin_dkv))
-        for s in range(NSEG)
-    ).astype(BF16)
-    page_grad = (
-        page_grad.reshape(pages_here, 2, HEAD_DIM, lay.pieces, lay.mem_pad)
-        .transpose(0, 3, 1, 2, 4)
-        .reshape(half, 2, HEAD_DIM, lay.mem_pad)
-    )
-    cross_dq_tokens, memory_grad = exchange(
-        5, [lay.from_units(all_parts(cross_dq)), lay.memory_from_units(page_grad)]
-    )
-    cross_dq = pick_part(cross_dq_tokens)[0]
-    if parts > 1:
-        memory_grad = jnp.sum(memory_grad.astype(F32), axis=0).astype(BF16)
-    else:
-        memory_grad = memory_grad[0]
-    dkc, dvc = memory_grad[0], memory_grad[1]
-    grad_memory = tp_total(dot(dkc, cross_key, 0, 1) + dot(dvc, cross_value, 0, 1))
-    grad_memory = grad_memory[: lay.mem_rows]
-
-    grad_hidden = tp_total(dot(cross_dq, cross_query, 0, 1))
-    grad_one = grad_two + norm_back(grad_hidden, unit_two, inv_two, gain_two)
-
-    self_in = grad_one.astype(BF16)
-    mixed_grad = dot(weight_out, self_in, 1, 1).astype(BF16)[None]
-    (mixed_grad,) = exchange(6, [lay.to_units(mixed_grad)])
-    middle_share = reduce_scatter(
-        jnp.concatenate(
-            [
-                dot(cross_in, cross_mixed, 0, 1),
-                dot(hidden_two, cross_dq, 0, 1),
-                dot(memory_padded, dkc, 0, 1),
-                dot(memory_padded, dvc, 0, 1),
-                dot(self_in, mixed, 0, 1),
-            ],
-            axis=1,
-        ),
-        count,
-        place,
-    )
-    dq, dkv = self_backward(
-        query,
-        qkv,
-        key_codes,
-        query_segments,
-        query_positions,
-        own_part(mixed_grad),
-        attention,
-        attention_log,
-        parts,
-    )
-    (dqkv,) = exchange(7, [lay.from_units(jnp.concatenate([all_parts(dq), dkv], axis=0))])
-    if parts > 1:
-        dkv = jnp.sum(dqkv[:, 1:].astype(F32), axis=0).astype(BF16)
-        dq, dk, dv = pick_part(dqkv)[0], dkv[0], dkv[1]
-    else:
-        dq, dk, dv = dqkv[0, 0], dqkv[0, 1], dqkv[0, 2]
-    grad_hidden = tp_total(
-        dot(dq, weight_query, 0, 1) + dot(dk, weight_key, 0, 1) + dot(dv, weight_value, 0, 1)
-    )
-    grad_input = grad_one + norm_back(grad_hidden, unit_one, inv_one, gain_one)
-    grad_input = grad_input.reshape(packs, rows, width)
-    first_share = reduce_scatter(
-        jnp.concatenate([dot(hidden_one, d, 0, 1) for d in (dq, dk, dv)], axis=1), count, place
-    )
-
-    ff, wide = weight_up.shape[1], weight_query.shape[1]
-    grad_down, grad_up = feed_share[:, :ff].T, feed_share[:, ff:]
-    middle = [middle_share[:, i * wide : (i + 1) * wide] for i in range(5)]
-    first = [first_share[:, i * wide : (i + 1) * wide] for i in range(3)]
+
+    middle = [columns_of(middle_share, i) for i in range(5)]
+    first = [columns_of(first_share, i) for i in range(3)]
 
     def own_rows(weight):
         return lax.dynamic_slice_in_dim(weight, place * share, share, 0).astype(F32)
@@ -741,10 +1100,10 @@
         first[0],
         first[1],
         first[2],
-        middle[4].T,
+        middle[2].T,
         middle[1],
-        middle[2],
         middle[3],
+        middle[4],
         middle[0].T,
         grad_up,
         grad_down,

time: 592 us -> 417 us (0.70)
  waiting for transfers between devices: 139 us -> 19.5 us
  Pallas kernels: 217 us -> 312 us
  local copies, waits for them, and re-layouts: 79.6 us -> 17.2 us
  other arithmetic: 67.6 us -> 36.5 us
  starting transfers between devices: 30.5 us -> 1.78 us
  matrix products: 45.4 us -> 17.5 us
    pallas_call x2 -> x1, Pallas kernels: 22 us -> 222 us  [backward(): pl.pallas_call(functools.partial(backward_body, lay, names, late, list(sc...]
    ppermute x25 -> x1, waiting for transfers between devices: 138 us -> 0.01 us  [local(): lax.ppermute(own_pages, 'blk', [(i, (i + count // packs) % count) for i i...]
    pallas_call x8 -> x4, Pallas kernels: 178 us -> 73.4 us  [exchange(): pl.pallas_call(body, out_shape=[jax.ShapeDtypeStruct(item[1], item[0].dty...]
    concatenate x3 -> x0, local copies, waits for them, and re-layouts: 35.5 us -> none  [the longest x1 17.5 us: local(): jnp.concatenate([dot(down_in, gelu_low, 0, 0), dot(hidden_three, up_grad,...]
    ppermute x25 -> x1, starting transfers between devices: 29.1 us -> 0.01 us  [local(): lax.ppermute(own_pages, 'blk', [(i, (i + count // packs) % count) for i i...]
    dot_general x30 -> x12, matrix products: 45.4 us -> 17.5 us  [dot(): lax.dot_general(left, right, (((contract_left,), (contract_right,)), ((),...]
    add x26 -> x2, other arithmetic: 21.9 us -> 1.9 us  [the longest x1 1.89 us: local(): memory_own.astype(F32) + memory_other.astype(F32)]
    ppermute x1, waiting for transfers between devices: 0.01 us -> 19.3 us  [local(): kv_twin = lax.ppermute(pages_of(twin_pages), 'blk', twin_pairs)]
  transfers between devices with their start and end apart: 34 -> 7, of which waited for: 14 -> 2; matrix products, arithmetic and copies ran while one was open for 25% -> 5% of each run, Pallas kernels for 25% -> 5%
where the time goes in v2:
time: 417 us; the launch traced here: 411 us
  Pallas kernels  312 us (75%)
  other arithmetic  36.5 us (9%)
  waiting for transfers between devices  19.5 us (5%)
  matrix products  17.5 us (4%)
  local copies, waits for them, and re-layouts  17.2 us (4%)
  between operations  6.36 us (2%)
    pallas_call x1, Pallas kernels, backward(): pl.pallas_call(functools.partial(backward_body, lay, names, late, list(sc...  222 us
    pallas_call x4, Pallas kernels, exchange(): pl.pallas_call(body, out_shape=[jax.ShapeDtypeStruct(item[1], item[0].dty...  73.4 us
    ppermute x1, waiting for transfers between devices, local(): kv_twin = lax.ppermute(pages_of(twin_pages), 'blk', twin_pairs)  19.3 us
    dot_general x12, matrix products, dot(): lax.dot_general(left, right, (((contract_left,), (contract_right,)), ((),...  17.5 us
    pallas_call x1, Pallas kernels, self_forward(): pl.pallas_call(functools.partial(self_forward_body, block, parts), grid=(...  9.14 us
  transfers between devices with their start and end apart: 7, of which 2 were waited for; matrix products, arithmetic and copies ran while one was open for 5% of the time, Pallas kernels for 5%

profile of v2, /device:TPU:0, one launch (start us, length us, event | category | flops | bytes accessed | tf_op | source)
XLA Modules:
  0.0 411.1 jit_solution(7506405038353739133)
XLA Ops:
  0.7 1.3 convert_reduce_fusion
  2.0 1.3 fusion.13
  3.3 2.4 fusion.14
  5.7 0.5 fusion.10
  6.3 0.5 fusion.9
  7.1 0.5 fusion.8
  8.0 1.0 fusion.7
  9.2 1.0 fusion.6
  10.3 1.2 pad_maximum_fusion.refs_2_
  11.5 1.0 pad_maximum_fusion.1.refs_0_
  12.5 0.6 broadcast_in_dim.20.refs_1_
  13.1 39.4 %shard_map.306 = (bf16[3,64,2048]{2,1,0:T(8,128)(2,1)}, s32[8,2048]{1,0:T(8,128)}, bf16[8,2,64,640]{3,2,1,0:T(8,128)(2,1)}) custom-call(bf16[3,512,256]{2,1,0:T(8,128)(2,1)} %pad_maximum_fusion.1.refs_0_, s32[2,8,128]{2,1,0:T(8,128)} %broadcast_in_dim.20.refs_1_, bf16[2,512,640]{2,1,0:T(8,128)(2,1)} %pad_maximum_fusion.refs_2_), custom_call_target="tpu_custom_call" | custom-call | tf_op jit(solution)/shard_map/pallas_call | solution.py:69
  52.4 0.8 slice_shift-right-arithmetic_fusion.qseg_ref
  53.4 0.8 iota_reduce_fusion
  55.1 0.6 fusion.31
  55.7 0.5 broadcast.175
  56.2 2.8 fusion.26
  59.0 1.3 copy.55.code_ref
  60.3 0.6 iota.17.qpos_ref
  61.0 9.1 %shard_map.307 = (f32[64,2048]{1,0:T(8,128)}, bf16[1,64,2048]{2,1,0:T(8,128)(2,1)}, f32[1,2048]{1,0:T(1,128)}) custom-call(bf16[3,64,2048]{2,1,0:T(8,128)(2,1)} %get-tuple-element.32.q_ref.k_ref.v_ref.refs_24_, bf16[3,64,2048]{2,1,0:T(8,128)(2,1)} %get-tuple-element.32.q_ref.k_ref.v_ref.refs_24_, ...), custom_call_target="tpu_custom_call" | custom-call | tf_op jit(solution)/shard_map/pallas_call | solution.py:206
  70.1 12.9 %shard_map.308 = bf16[1,1,512,256]{3,2,1,0:T(8,128)(2,1)} custom-call(bf16[1,64,2048]{2,1,0:T(8,128)(2,1)} %get-tuple-element.34.refs_0_), custom_call_target="tpu_custom_call" | custom-call | tf_op jit(solution)/shard_map/pallas_call | solution.py:69
  85.1 0.6 fusion.32
  87.6 1.4 constant_dynamic-slice_fusion.5
  89.1 0.9 collective-permute-start.2
  90.0 0.5 convolution_convert_fusion.3
  90.6 0.7 fusion.25
  91.3 19.3 %collective-permute-done.2 = bf16[3,2,64,640]{3,2,1,0:T(8,128)(2,1)} collective-permute-done((bf16[3,2,64,640]{3,2,1,0:T(8,128)(2,1)S(1)}, bf16[3,2,64,640]{3,2,1,0:T(8,128)(2,1)}, u32[]{:S(2)}, u32[]{:S(2)}) %collective-permute-start.2) | collective-permute-done | bytes 491552 | tf_op jit(solution)/shard_map/ppermute | solution.py:987
  110.6 2.0 maximum_select_fusion.kv_ref.refs_16_
  113.3 1.3 multiply_convert_fusion.2
  114.6 0.8 copy-done.3
  115.4 1.2 fusion.11.refs_0_
  116.6 11.0 %shard_map.309.q_ref.refs_17_ = bf16[1,64,2048]{2,1,0:T(8,128)(2,1)} custom-call(bf16[1,512,256]{2,1,0:T(8,128)(2,1)} %fusion.11.refs_0_), custom_call_target="tpu_custom_call" | custom-call | tf_op jit(solution)/shard_map/pallas_call | solution.py:69
  127.7 7.8 %shard_map.310 = (f32[64,2048]{1,0:T(8,128)}, bf16[1,64,2048]{2,1,0:T(8,128)(2,1)}, f32[1,2048]{1,0:T(1,128)}) custom-call(s32[4]{0:T(128)} %get-tuple-element.51.low_ref, s32[4]{0:T(128)} %get-tuple-element.50.high_ref, bf16[1,64,2048]{2,1,0:T(8,128)(2,1)} %shard_map.309.q_ref.refs_17_, bf16[3,2,64,640]{3,2,1,0:T(8,128)(2,1)} %maximum_select_fusion.kv_ref.refs_16_, ...), custom_call_target="tpu_custom_call" | custom-call | tf_op jit(solution)/shard_map/pallas_call | solution.py:276
  135.4 10.1 %shard_map.311 = bf16[1,1,512,256]{3,2,1,0:T(8,128)(2,1)} custom-call(bf16[1,64,2048]{2,1,0:T(8,128)(2,1)} %get-tuple-element.37.refs_0_), custom_call_target="tpu_custom_call" | custom-call | tf_op jit(solution)/shard_map/pallas_call | solution.py:69
  145.6 1.4 convolution_convert_fusion.2
  147.1 0.8 copy.58.refs_4_
  147.9 2.5 pad.4.refs_25_
  150.3 0.8 dynamic-slice_bitcast_fusion.2
  151.2 1.6 fusion.29
  153.5 1.3 fusion.35
  154.9 1.2 copy-done.29
  156.1 6.8 %add_convert_fusion = (bf16[256,2048]{1,0:T(8,128)(2,1)S(1)}, f32[256,2048]{1,0:T(8,128)S(1)}) fusion(f32[256,2048]{1,0:T(8,128)S(1)} %fusion.35, bf16[256,1024]{1,0:T(8,128)(2,1)S(1)} %bitcast.154, bf16[2048,1024]{1,0:T(8,128)(2,1)S(1)} %copy-done.29), kind=kOutput, calls=%fused_computation.3 | convolution fusion | flops 1111490560 | bytes 9961472 | tf_op jit(solution)/shard_map/dot_general | solution.py:25
  162.9 1.3 convolution_convert_fusion.4
  164.2 0.6 collective-permute-start.5
  164.7 0.4 multiply_convert_fusion.refs_13_
  165.1 1.3 convolution_convert_fusion.5
  166.5 0.7 compare_convert_fusion.refs_0_
  167.2 0.8 copy.57.refs_2_
  168.0 0.4 fusion.15
  168.5 3.0 fusion.27
  171.6 222.0 %shard_map.312 = (f32[256,1024]{1,0:T(8,128)}, bf16[640,1024]{1,0:T(8,128)(2,1)}, bf16[640,1024]{1,0:T(8,128)(2,1)}, f32[2,64,2048]{2,1,0:T(8,128)}, f32[2,64,1280]{2,1,0:T(8,128)}, /*index=5*/f32[2,64,768]{2,1,0:T(8,128)}) custom-call(f32[2,3,8]{2,1,0:T(4,128)} %compare_convert_fusion.refs_0_, bf16[256,1024]{1,0:T(8,128)(2,1)} %get-tuple-element.64.refs_1_, ...), custom_call_target="tpu_custom_call" | custom-call | tf_op jit(solution)/shard_map/pallas_call | solution.py:847
  393.6 2.1 multiply_reduce_fusion.3
  395.7 2.0 slice_bitcast_fusion
  397.9 1.6 multiply_reduce_fusion.7
  399.5 1.6 multiply_reduce_fusion.6
  401.1 1.6 multiply_reduce_fusion.5
  402.7 1.6 multiply_reduce_fusion.4
  404.5 1.9 convert_add_fusion
  406.4 0.7 maximum_bitcast_fusion
  407.1 0.7 pad_maximum_fusion.7
  407.7 0.7 pad_maximum_fusion.8
  408.4 0.7 maximum_bitcast_fusion.1
  409.1 0.5 slice_bitcast_fusion.18
  409.6 1.0 copy.66
  (95 shorter events, 3.2 us)
Async XLA Ops:
  0.6 54.3 %copy-start = (s32[2,3]{1,0:T(2,128)S(1)}, s32[2,3]{1,0:T(2,128)}, u32[]{:S(2)}) copy-start(s32[2,3]{1,0:T(2,128)} %param.23) | copy-start | bytes 76
  0.7 5.1 %copy-start.6 = (bf16[1024,512]{1,0:T(8,128)(2,1)S(1)}, bf16[1024,512]{1,0:T(8,128)(2,1)}, u32[]{:S(2)}) copy-start(bf16[1024,512]{1,0:T(8,128)(2,1)} %refs_31_.1) | copy-start | bytes 3145732
  3.3 3.0 copy-start.5
  5.7 2.0 copy-start.2
  5.7 1.4 copy-start.4
  6.3 1.4 copy-start.14
  6.3 1.7 copy-start.17
  8.0 1.2 copy-start.18
  9.2 1.1 copy-start.27
  9.2 1.1 copy-start.28
  53.3 7.7 %copy-start.23 = (s32[1,2048]{1,0:T(1,128)}, s32[1,2048]{1,0:T(1,128)S(1)}, u32[]{:S(2)}) copy-start(s32[1,2048]{1,0:T(1,128)S(1)} %slice_shift-right-arithmetic_fusion.qseg_ref) | copy-start | bytes 24580
  55.1 29.9 %collective-permute-start.1 = (s32[3]{0:T(128)S(1)}, s32[3]{0:T(128)S(1)}, u32[]{:S(2)}, u32[]{:S(2)}) collective-permute-start(s32[3]{0:T(128)S(1)} %get-tuple-element.71), channel_id=1, source_target_pairs={{0,16},{2,18},{4,20},{6,22},{8,24},{10,26},{12,28},{14,30},{16,0},... | collective-permute-start | bytes 44 | tf_op jit(solution)/shard_map/ppermute | solution.py:971
  70.1 19.9 %copy-start.10 = (bf16[512,1024]{1,0:T(8,128)(2,1)S(1)}, bf16[512,1024]{1,0:T(8,128)(2,1)}, u32[]{:S(2)}) copy-start(bf16[512,1024]{1,0:T(8,128)(2,1)} %refs_28_.1) | copy-start | bytes 3145732
  83.0 7.0 %copy-start.11 = (bf16[1,1,512,256]{3,2,1,0:T(8,128)(2,1)S(1)}, bf16[1,1,512,256]{3,2,1,0:T(8,128)(2,1)}, u32[]{:S(2)}) copy-start(bf16[1,1,512,256]{3,2,1,0:T(8,128)(2,1)} %shard_map.308) | copy-start | bytes 786436
  89.0 23.6 %copy-start.1 = (bf16[2,128,1024]{2,1,0:T(8,128)(2,1)S(1)}, bf16[2,128,1024]{2,1,0:T(8,128)(2,1)}, u32[]{:S(2)}) copy-start(bf16[2,128,1024]{2,1,0:T(8,128)(2,1)} %param.19) | copy-start | bytes 1572868
  89.1 21.5 %collective-permute-start.2 = (bf16[3,2,64,640]{3,2,1,0:T(8,128)(2,1)S(1)}, bf16[3,2,64,640]{3,2,1,0:T(8,128)(2,1)}, u32[]{:S(2)}, u32[]{:S(2)}) collective-permute-start(bf16[3,2,64,640]{3,2,1,0:T(8,128)(2,1)S(1)} %pad_maximum_fusion.2), channel_id=1, source_target_pairs={{0,16},{2,18},{4,20},{6,22},{8,24},{10,26},{12,28},{14,30},{16,0},... | collective-permute-start | bytes 1474568 | tf_op jit(solution)/shard_map/ppermute | solution.py:987
  90.5 22.1 %collective-permute-start = (bf16[256,1024]{1,0:T(8,128)(2,1)S(1)}, bf16[256,1024]{1,0:T(8,128)(2,1)S(1)}, u32[]{:S(2)}, u32[]{:S(2)}) collective-permute-start(bf16[256,1024]{1,0:T(8,128)(2,1)S(1)} %convolution_convert_fusion.3), channel_id=1, source_target_pairs={{0,1},{1,0},{2,3},{3,2},{4,5},{5,4},{6,7},{7,6},{8,9},{9,8},{10,11... | collective-permute-start | bytes 1572872 | tf_op jit(solution)/shard_map/ppermute | solution.py:883
  110.6 2.7 copy-start.25
  112.9 2.5 copy-start.7
  114.6 0.8 copy-start.3
  114.6 31.0 %copy-start.9 = (bf16[512,1024]{1,0:T(8,128)(2,1)S(1)}, bf16[512,1024]{1,0:T(8,128)(2,1)}, u32[]{:S(2)}) copy-start(bf16[512,1024]{1,0:T(8,128)(2,1)} %refs_11_.1) | copy-start | bytes 3145732
  145.6 5.5 %copy-start.24 = (f32[1024]{0:T(1024)S(1)}, f32[1024]{0:T(1024)}, u32[]{:S(2)}) copy-start(f32[1024]{0:T(1024)} %param.34) | copy-start | bytes 12292
  147.0 4.2 %collective-permute-start.3 = (bf16[256,1024]{1,0:T(8,128)(2,1)S(1)}, bf16[256,1024]{1,0:T(8,128)(2,1)}, u32[]{:S(2)}, u32[]{:S(2)}) collective-permute-start(bf16[256,1024]{1,0:T(8,128)(2,1)S(1)} %convolution_convert_fusion.2), channel_id=1, source_target_pairs={{0,1},{1,0},{2,3},{3,2},{4,5},{5,4},{6,7},{7,6},{8,9},{9,8},{10,11... | collective-permute-start | bytes 1572872 | tf_op jit(solution)/shard_map/ppermute | solution.py:883
  151.2 2.3 copy-start.26
  153.5 1.3 copy-start.12
  153.5 1.3 copy-start.13
  153.5 2.5 copy-start.29
  162.9 1.3 copy-start.19
  164.2 3.8 collective-permute-start.5
  165.1 1.3 copy-start.8
  166.4 2.1 collective-permute-start.4
  393.6 4.2 %copy-start.22 = (f32[2,64,768]{2,1,0:T(8,128)S(1)}, f32[2,64,768]{2,1,0:T(8,128)}, u32[]{:S(2)}) copy-start(f32[2,64,768]{2,1,0:T(8,128)} %get-tuple-element.45) | copy-start | bytes 1179652
  393.6 4.2 %copy-start.21 = (f32[2,64,1280]{2,1,0:T(8,128)S(1)}, f32[2,64,1280]{2,1,0:T(8,128)}, u32[]{:S(2)}) copy-start(f32[2,64,1280]{2,1,0:T(8,128)} %get-tuple-element.46) | copy-start | bytes 1966084
  395.7 8.7 %copy-start.15 = (bf16[640,1024]{1,0:T(8,128)(2,1)S(1)}, bf16[640,1024]{1,0:T(8,128)(2,1)}, u32[]{:S(2)}) copy-start(bf16[640,1024]{1,0:T(8,128)(2,1)} %get-tuple-element.43) | copy-start | bytes 3932164
  395.7 8.7 %copy-start.16 = (bf16[640,1024]{1,0:T(8,128)(2,1)S(1)}, bf16[640,1024]{1,0:T(8,128)(2,1)}, u32[]{:S(2)}) copy-start(bf16[640,1024]{1,0:T(8,128)(2,1)} %get-tuple-element.44) | copy-start | bytes 3932164
  404.4 4.7 %collective-permute-start.6 = (f32[3,64]{1,0:T(4,128)S(1)}, f32[3,64]{1,0:T(4,128)S(1)}, u32[]{:S(2)}, u32[]{:S(2)}) collective-permute-start(f32[3,64]{1,0:T(4,128)S(1)} %pad_maximum_fusion.9), channel_id=1, source_target_pairs={{0,1},{1,0},{2,3},{3,2},{4,5},{5,4},{6,7},{7,6},{8,9},{9,8},{10,11... | collective-permute-start | bytes 2312 | tf_op jit(solution)/shard_map/ppermute | solution.py:883
  404.5 5.1 %copy-start.20 = (f32[256,1024]{1,0:T(8,128)S(1)}, f32[256,1024]{1,0:T(8,128)}, u32[]{:S(2)}) copy-start(f32[256,1024]{1,0:T(8,128)} %get-tuple-element.42) | copy-start | bytes 3145732
